TPU v7x, 32 devices: a whole 2x2x4 slice. The times are simulated.
32 devices in a mesh: dp: 2 (over x), mp: 16 (over z, y, core).
Axes of the slice: x: 2, y: 2, z: 4, core: 2. Of those that a mesh axis runs over, the one named last changes fastest.
Arguments:
- tokens: bfloat16 [256, 8192], P('dp', 'mp'), may hold values from -6 to 6
- gate_weight: bfloat16 [8192, 14336], P('mp', 'dp'), may hold values from -0.0625 to 0.0625
- up_weight: bfloat16 [8192, 14336], P('mp', 'dp'), may hold values from -0.0625 to 0.0625
- down_weight: bfloat16 [14336, 8192], P('dp', 'mp'), may hold values from -0.046875 to 0.046875
- factor_self: bfloat16 [5, 8192, 256], P(None, 'mp'), may hold values from -0.25 to 0.25
- factor_cross: bfloat16 [5, 8192, 256], P(None, 'mp'), may hold values from -0.25 to 0.25
- cotangent: bfloat16 [256, 8192], P('dp', 'mp'), may hold values from -1.1953125 to 1.1953125
Outputs:
- mixed_out: bfloat16 [256, 8192], P('dp', 'mp')
- input_grad: bfloat16 [256, 8192], P('dp', 'mp')
- self_grad: float32 [5, 8192, 256], P(None, 'mp')
- cross_grad: float32 [5, 8192, 256], P(None, 'mp')
All inputs are finite; a program needn't handle non-finite values.
Results may differ from a plain program's by a relative error of at most 0.04.
Values may be sent and summed in bfloat16 or wider, within the bound.
A program may use at most 128 MiB of HBM per device.

v0:
```python
import jax
import jax.numpy as jnp
from jax import lax
from jax.sharding import PartitionSpec as P

BLOCK = 256
SECTIONS = 5


def swapped(block, axis, stride):
    count = lax.axis_size(axis)
    route = []
    for low in range(count):
        high = low | 1 << stride
        if high != low and high < count:
            route += [(low, high), (high, low)]
    return lax.ppermute(block, axis, route)


def local_partner(blocks, degree):
    tok_rows, amount, breadth = blocks.shape
    distance = 2**degree
    folded = blocks.reshape(tok_rows, amount // (2 * distance), 2, distance, breadth)
    return jnp.flip(folded, 2).reshape(tok_rows, amount, breadth)


def contract_last(left_side, right_side):
    return lax.dot_general(
        left_side, right_side, (((1,), (1,)), ((), ())), preferred_element_type=jnp.float32
    )


def per_device(tokens, gate_weight, up_weight, down_weight, factor_self, factor_cross, cotangent):
    tok_rows, local_width = tokens.shape
    per_dev = local_width // BLOCK
    local_bits = per_dev.bit_length() - 1
    current = tokens.reshape(tok_rows, per_dev, BLOCK)
    inputs = []
    partners = []
    for degree in range(SECTIONS):
        self_mat = factor_self[degree].reshape(per_dev, BLOCK, BLOCK)
        cross_mat = factor_cross[degree].reshape(per_dev, BLOCK, BLOCK)
        if degree < local_bits:
            partner = local_partner(current, degree)
        else:
            partner = swapped(current, "mp", degree - local_bits)
        inputs.append(current)
        partners.append(partner)
        result = jnp.einsum("tkb,kbc->tkc", current, self_mat, preferred_element_type=jnp.float32)
        result = result + jnp.einsum(
            "tkb,kbc->tkc", partner, cross_mat, preferred_element_type=jnp.float32
        )
        current = result.astype(jnp.bfloat16)
    rotated = current.reshape(tok_rows, local_width)
    segment = lax.all_gather(rotated, "dp", axis=0, tiled=True)
    products = jnp.stack(
        [
            jnp.dot(segment, gate_weight, preferred_element_type=jnp.float32),
            jnp.dot(segment, up_weight, preferred_element_type=jnp.float32),
        ]
    )
    reduced = lax.psum_scatter(
        products.astype(jnp.bfloat16), "mp", scatter_dimension=1, tiled=True
    ).astype(jnp.float32)
    gate_sum = reduced[0]
    up_sum = reduced[1]
    hidden = (jax.nn.silu(gate_sum) * up_sum).astype(jnp.bfloat16)
    partial_value = jnp.dot(
        lax.all_gather(hidden, "mp", axis=0, tiled=True),
        down_weight,
        preferred_element_type=jnp.float32,
    )
    mixed_out = lax.psum_scatter(
        partial_value.astype(jnp.bfloat16), "dp", scatter_dimension=0, tiled=True
    )
    hidden_terms = contract_last(lax.all_gather(cotangent, "dp", axis=0, tiled=True), down_weight)
    hidden_grad = lax.psum_scatter(
        hidden_terms.astype(jnp.bfloat16), "mp", scatter_dimension=0, tiled=True
    ).astype(jnp.float32)
    logistic = jax.nn.sigmoid(gate_sum)
    gate_grad = (hidden_grad * up_sum * logistic * (1.0 + gate_sum * (1.0 - logistic))).astype(
        jnp.bfloat16
    )
    up_grad = (hidden_grad * gate_sum * logistic).astype(jnp.bfloat16)
    stacked = jnp.stack([gate_grad, up_grad])
    segment = lax.all_gather(stacked, "mp", axis=1, tiled=True)
    rot_terms = contract_last(segment[0], gate_weight) + contract_last(segment[1], up_weight)
    gradient = lax.psum_scatter(
        rot_terms.astype(jnp.bfloat16), "dp", scatter_dimension=0, tiled=True
    )
    gradient = gradient.reshape(tok_rows, per_dev, BLOCK)
    self_list = [None] * SECTIONS
    cross_list = [None] * SECTIONS
    for degree in reversed(range(SECTIONS)):
        self_mat = factor_self[degree].reshape(per_dev, BLOCK, BLOCK)
        cross_mat = factor_cross[degree].reshape(per_dev, BLOCK, BLOCK)
        self_part = jnp.einsum(
            "tkb,tkc->kbc", inputs[degree], gradient, preferred_element_type=jnp.float32
        )
        cross_part = jnp.einsum(
            "tkb,tkc->kbc", partners[degree], gradient, preferred_element_type=jnp.float32
        )
        self_part, cross_part = (
            lax.psum(self_part.astype(jnp.bfloat16), "dp").astype(jnp.float32),
            lax.psum(cross_part.astype(jnp.bfloat16), "dp").astype(jnp.float32),
        )
        self_list[degree] = self_part.reshape(per_dev * BLOCK, BLOCK)
        cross_list[degree] = cross_part.reshape(per_dev * BLOCK, BLOCK)
        direct = jnp.einsum("tkc,kbc->tkb", gradient, self_mat, preferred_element_type=jnp.float32)
        carried = jnp.einsum(
            "tkc,kbc->tkb", gradient, cross_mat, preferred_element_type=jnp.float32
        )
        if degree < local_bits:
            returned = local_partner(carried, degree)
        else:
            returned = swapped(carried.astype(jnp.bfloat16), "mp", degree - local_bits).astype(
                carried.dtype
            )
        gradient = (direct + returned).astype(jnp.bfloat16)
    self_grad = jnp.stack(self_list)
    cross_grad = jnp.stack(cross_list)
    return (mixed_out, gradient.reshape(tok_rows, local_width), self_grad, cross_grad)


def solution(mesh):
    return jax.shard_map(
        per_device,
        mesh=mesh,
        in_specs=(
            P("dp", "mp"),
            P("mp", "dp"),
            P("mp", "dp"),
            P("dp", "mp"),
            P(None, "mp", None),
            P(None, "mp", None),
            P("dp", "mp"),
        ),
        out_specs=(P("dp", "mp"), P("dp", "mp"), P(None, "mp", None), P(None, "mp", None)),
        check_vma=False,
    )
```

profile of v0, /device:TPU:0, one launch (start us, length us, event | category | flops | bytes accessed | tf_op | source)
XLA Modules:
  0.0 463.3 jit_solution(16003903176202718582)
XLA Ops:
  7.2 1.4 fusion.48
  8.6 1.0 copy.62
  9.6 1.4 fusion.47
  13.4 2.9 collective-permute-start.1
  16.5 3.6 collective-permute-done.1
  20.3 1.9 collective-permute-start.2
  22.4 3.0 collective-permute-done.2
  25.7 2.8 collective-permute-start.3
  28.6 4.9 %collective-permute-done.3 = bf16[128,2,256]{2,0,1:T(8,128)(2,1)S(1)} collective-permute-done((bf16[128,2,256]{2,0,1:T(8,128)(2,1)S(1)}, bf16[128,2,256]{2,0,1:T(8,128)(2,1)S(1)}, u32[]{:S(2)}, u32[]{:S(2)}) %collective-permute-start.3) | collective-permute-done | bytes 131104 | tf_op jit(solution)/shard_map/ppermute | solution.py:17
  34.6 5.7 %all_gather.12 = bf16[256,512]{0,1:T(8,128)(2,1)S(1)} all-gather(bf16[128,512]{0,1:T(8,128)(2,1)S(1)} %bitcast.232), channel_id=1, replica_groups=mesh['dp'=2,'mp'=16] {'dp'}, dimensions={0}, use_global_device_ids=true | all-gather | bytes 393216 | tf_op jit(solution)/shard_map/all_gather | solution.py:55
  40.2 5.2 %fusion = bf16[1,256,7168]{2,1,0:T(8,128)(2,1)S(1)} fusion(bf16[256,512]{0,1:T(8,128)(2,1)S(1)} %all_gather.12, bf16[512,7168]{1,0:T(8,128)(2,1)} %param.8), kind=kOutput, calls=%fused_computation.3 | convolution fusion | flops 1880883200 | bytes 11272192 | tf_op jit(solution)/shard_map/dot_general | solution.py:58
  45.4 5.2 %fusion.1 = bf16[1,256,7168]{2,1,0:T(8,128)(2,1)S(1)} fusion(bf16[256,512]{0,1:T(8,128)(2,1)S(1)} %all_gather.12, bf16[512,7168]{1,0:T(8,128)(2,1)} %param.9), kind=kOutput, calls=%fused_computation.4 | convolution fusion | flops 1880883200 | bytes 11272192 | tf_op jit(solution)/shard_map/dot_general | solution.py:59
  50.6 3.5 pad_maximum_fusion
  55.0 5.6 %all_gather.14 = bf16[256,512]{1,0:T(8,128)(2,1)S(1)} all-gather(bf16[128,512]{1,0:T(8,128)(2,1)S(1)} %copy-done.23), channel_id=1, replica_groups=mesh['dp'=2,'mp'=16] {'dp'}, dimensions={0}, use_global_device_ids=true | all-gather | bytes 393216 | tf_op jit(solution)/shard_map/all_gather | solution.py:76
  60.6 7.8 %convolution_convert_fusion = bf16[256,7168]{1,0:T(8,128)(2,1)} fusion(bf16[256,512]{1,0:T(8,128)(2,1)S(1)} %all_gather.14, bf16[7168,512]{1,0:T(8,128)(2,1)} %param.10), kind=kOutput, calls=%fused_computation | convolution fusion | flops 1880883200 | bytes 11272192 | tf_op jit(solution)/shard_map/dot_general | solution.py:28
  68.5 78.1 %reduce-scatter.5.cloned.1.call-done = bf16[2,16,7168]{2,1,0:T(8,128)(2,1)} async-done(((bf16[2,256,7168]{2,1,0:T(8,128)(2,1)}), bf16[2,16,7168]{2,1,0:T(8,128)(2,1)}) %reduce-scatter.5.cloned.1.call-update) | async-done | bytes 458768 | tf_op jit(solution)/shard_map/reduce_scatter | solution.py:62
  146.6 1.1 convert_element_type.162
  147.7 71.1 %reduce-scatter.9.cloned.1.call-done = bf16[16,7168]{1,0:T(8,128)(2,1)} async-done(((bf16[256,7168]{1,0:T(8,128)(2,1)}), bf16[16,7168]{1,0:T(8,128)(2,1)}) %reduce-scatter.9.cloned.1.call-update) | async-done | bytes 229392 | tf_op jit(solution)/shard_map/reduce_scatter | solution.py:77
  218.8 1.9 fusion.34
  221.7 67.3 %all-gather.5.cloned.1.call-done = bf16[2,256,7168]{2,1,0:T(8,128)(2,1)} async-done(((bf16[2,16,7168]{2,1,0:T(8,128)(2,1)}), bf16[2,256,7168]{2,1,0:T(8,128)(2,1)}) %all-gather.5.cloned.1.call-update) | async-done | bytes 7340048 | tf_op jit(solution)/shard_map/all_gather | solution.py:86
  289.1 6.4 %fusion.2 = f32[256,512]{1,0:T(8,128)S(1)} fusion(bf16[512,7168]{1,0:T(8,128)(2,1)} %param.9, bf16[2,256,7168]{2,1,0:T(8,128)(2,1)} %all-gather.5.cloned.1.call-done), kind=kOutput, calls=%fused_computation.7 | convolution fusion | flops 1879048192 | bytes 11534336 | tf_op jit(solution)/shard_map/dot_general | solution.py:28
  295.5 5.9 %fusion.5 = bf16[256,512]{1,0:T(8,128)(2,1)} fusion(f32[256,512]{1,0:T(8,128)S(1)} %fusion.2, bf16[512,7168]{1,0:T(8,128)(2,1)} %param.8, bf16[2,256,7168]{2,1,0:T(8,128)(2,1)S(1)} %copy-done.24), kind=kOutput, calls=%fused_computation.22 | convolution fusion | flops 1879310336 | bytes 11796480 | tf_op jit(solution)/shard_map/dot_general | solution.py:28
  302.1 9.6 %reduce-scatter.11.cloned.1.call-done = bf16[128,512]{1,0:T(8,128)(2,1)} async-done(((bf16[256,512]{1,0:T(8,128)(2,1)}), bf16[128,512]{1,0:T(8,128)(2,1)}) %reduce-scatter.11.cloned.1.call-update) | async-done | bytes 131088 | tf_op jit(solution)/shard_map/reduce_scatter | solution.py:88
  311.7 1.1 fusion.19
  312.9 2.5 collective-permute-start.4
  315.4 1.9 convolution_convert_fusion.9
  317.2 1.9 convolution_convert_fusion.5
  319.1 2.8 collective-permute-done.4
  321.9 1.1 add_convert_fusion
  323.8 1.0 convolution_convert_fusion.10
  324.8 1.0 convolution_convert_fusion.6
  325.8 5.9 %collective-permute-done.5 = bf16[128,2,256]{2,0,1:T(8,128)(2,1)S(1)} collective-permute-done((bf16[128,2,256]{2,0,1:T(8,128)(2,1)S(1)}, bf16[128,2,256]{2,0,1:T(8,128)(2,1)S(1)}, u32[]{:S(2)}, u32[]{:S(2)}) %collective-permute-start.5) | collective-permute-done | bytes 131104 | tf_op jit(solution)/shard_map/ppermute | solution.py:17
  332.2 1.5 collective-permute-start.6
  333.7 1.0 convolution_convert_fusion.11
  334.7 1.0 convolution_convert_fusion.7
  335.7 1.8 collective-permute-done.6
  342.0 21.5 %all-gather.3.cloned.1.call-done = bf16[256,7168]{1,0:T(8,128)(2,1)} async-done(((bf16[16,7168]{1,0:T(8,128)(2,1)}), bf16[256,7168]{1,0:T(8,128)(2,1)}) %all-gather.3.cloned.1.call-update) | async-done | bytes 3670032 | tf_op jit(solution)/shard_map/all_gather | solution.py:69
  363.5 7.0 %convolution_convert_fusion.13 = bf16[256,512]{1,0:T(8,128)(2,1)} fusion(bf16[256,7168]{1,0:T(8,128)(2,1)} %all-gather.3.cloned.1.call-done, bf16[7168,512]{1,0:T(8,128)(2,1)} %param.10), kind=kOutput, calls=%fused_computation.21 | convolution fusion | flops 1879179264 | bytes 11272192 | tf_op jit(solution)/shard_map/dot_general | solution.py:68
  371.9 69.9 %all-reduce.3.cloned.1.call-done = (bf16[1,512,256]{2,1,0:T(8,128)(2,1)}, bf16[1,512,256]{2,1,0:T(8,128)(2,1)}, bf16[1,512,256]{2,1,0:T(8,128)(2,1)}, bf16[1,512...) async-done(((bf16[1,512,256]{2,1,0:T(8,128)(2,1)}, ...) | async-done | bytes 2621456 | tf_op jit(solution)/shard_map/psum | solution.py:104
  441.8 1.0 constant_dynamic-update-slice_fusion.9
  443.8 1.0 constant_dynamic-update-slice_fusion.8
  444.8 1.0 constant_dynamic-update-slice_fusion.7
  445.8 1.0 constant_dynamic-update-slice_fusion.6
  446.8 1.0 constant_dynamic-update-slice_fusion.3
  447.7 1.0 constant_dynamic-update-slice_fusion.2
  448.8 1.7 stack.40
  450.6 1.7 stack.42
  452.3 4.1 reduce-scatter.7.cloned.1.call-done
  (100 shorter events, 15.1 us)
Async XLA Ops:
  7.2 139.5 %reduce-scatter.5.cloned.1.call-start = ((), (), s32[]{:S(2)}) async-start(), calls=%async_computation.4 | async-start | bytes 7798784 | tf_op jit(solution)/shard_map/reduce_scatter | solution.py:62
  9.6 12.8 %copy-start = (bf16[128,512]{0,1:T(8,128)(2,1)}, bf16[128,512]{0,1:T(8,128)(2,1)S(1)}, u32[]{:S(2)}) copy-start(bf16[128,512]{0,1:T(8,128)(2,1)S(1)} %copy.62) | copy-start | bytes 393220
  11.0 23.5 %copy-start.10 = (bf16[128,1,2,1,256]{0,4,2,3,1:T(8,128)(2,1)}, bf16[128,1,2,1,256]{0,4,2,3,1:T(8,128)(2,1)S(1)}, u32[]{:S(2)}) copy-start(bf16[128,1,2,1,256]{0,4,2,3,1:T(8,128)(2,1)S(1)} %rev.6) | copy-start | bytes 393220
  11.6 13.8 %copy-start.2 = (bf16[128,2,256]{0,2,1:T(8,128)(2,1)}, bf16[128,2,256]{0,2,1:T(8,128)(2,1)S(1)}, u32[]{:S(2)}) copy-start(bf16[128,2,256]{0,2,1:T(8,128)(2,1)S(1)} %fusion.27) | copy-start | bytes 393220
  11.6 1.5 collective-permute-start
  13.1 3.2 copy-start.12
  13.4 12.1 %copy-start.4 = (bf16[128,2,256]{2,0,1:T(8,128)(2,1)}, bf16[128,2,256]{2,0,1:T(8,128)(2,1)S(1)}, u32[]{:S(2)}) copy-start(bf16[128,2,256]{2,0,1:T(8,128)(2,1)S(1)} %fusion.26) | copy-start | bytes 393220
  13.4 6.8 %collective-permute-start.1 = (bf16[128,2,256]{2,0,1:T(8,128)(2,1)S(1)}, bf16[128,2,256]{2,0,1:T(8,128)(2,1)S(1)}, u32[]{:S(2)}, u32[]{:S(2)}) collective-permute-start(bf16[128,2,256]{2,0,1:T(8,128)(2,1)S(1)} %fusion.26), channel_id=1, source_target_pairs={{0,2},{2,0},{1,3},{3,1},{4,6},{6,4},{5,7},{7,5},{8,10},{10,8},{9,1... | collective-permute-start | bytes 393224 | tf_op jit(solution)/shard_map/ppermute | solution.py:17
  20.1 13.5 %copy-start.14 = (bf16[128,2,256]{2,0,1:T(8,128)(2,1)}, bf16[128,2,256]{2,0,1:T(8,128)(2,1)S(1)}, u32[]{:S(2)}) copy-start(bf16[128,2,256]{2,0,1:T(8,128)(2,1)S(1)} %collective-permute-done.1) | copy-start | bytes 393220
  20.3 5.1 %copy-start.6 = (bf16[128,2,256]{2,0,1:T(8,128)(2,1)}, bf16[128,2,256]{2,0,1:T(8,128)(2,1)S(1)}, u32[]{:S(2)}) copy-start(bf16[128,2,256]{2,0,1:T(8,128)(2,1)S(1)} %fusion.25) | copy-start | bytes 393220
  20.3 5.1 %collective-permute-start.2 = (bf16[128,2,256]{2,0,1:T(8,128)(2,1)S(1)}, bf16[128,2,256]{2,0,1:T(8,128)(2,1)S(1)}, u32[]{:S(2)}, u32[]{:S(2)}) collective-permute-start(bf16[128,2,256]{2,0,1:T(8,128)(2,1)S(1)} %fusion.25), channel_id=1, source_target_pairs={{0,4},{4,0},{1,5},{5,1},{2,6},{6,2},{3,7},{7,3},{8,12},{12,8},{9,1... | collective-permute-start | bytes 393224 | tf_op jit(solution)/shard_map/ppermute | solution.py:17
  25.4 8.1 %copy-start.16 = (bf16[128,2,256]{2,0,1:T(8,128)(2,1)}, bf16[128,2,256]{2,0,1:T(8,128)(2,1)S(1)}, u32[]{:S(2)}) copy-start(bf16[128,2,256]{2,0,1:T(8,128)(2,1)S(1)} %collective-permute-done.2) | copy-start | bytes 393220
  25.6 2.8 copy-start.8
  25.7 7.9 %collective-permute-start.3 = (bf16[128,2,256]{2,0,1:T(8,128)(2,1)S(1)}, bf16[128,2,256]{2,0,1:T(8,128)(2,1)S(1)}, u32[]{:S(2)}, u32[]{:S(2)}) collective-permute-start(bf16[128,2,256]{2,0,1:T(8,128)(2,1)S(1)} %fusion.24), channel_id=1, source_target_pairs={{0,8},{8,0},{1,9},{9,1},{2,10},{10,2},{3,11},{11,3},{4,12},{12,4},... | collective-permute-start | bytes 393224 | tf_op jit(solution)/shard_map/ppermute | solution.py:17
  33.6 0.7 copy-start.18
  54.1 0.9 copy-start.23
  54.1 164.7 %reduce-scatter.9.cloned.1.call-start = ((), (), s32[]{:S(2)}) async-start(), calls=%async_computation.7 | async-start | bytes 3899392 | tf_op jit(solution)/shard_map/reduce_scatter | solution.py:77
  68.4 220.6 %all-gather.5.cloned.1.call-start = ((), (), s32[]{:S(2)}) async-start(), calls=%async_computation.8 | async-start | bytes 7798784 | tf_op jit(solution)/shard_map/all_gather | solution.py:86
  221.5 90.2 %reduce-scatter.11.cloned.1.call-start = ((), (), s32[]{:S(2)}) async-start(), calls=%async_computation.9 | async-start | bytes 393216 | tf_op jit(solution)/shard_map/reduce_scatter | solution.py:88
  289.1 6.4 %copy-start.24 = (bf16[2,256,7168]{2,1,0:T(8,128)(2,1)S(1)}, bf16[2,256,7168]{2,1,0:T(8,128)(2,1)}, u32[]{:S(2)}) copy-start(bf16[2,256,7168]{2,1,0:T(8,128)(2,1)} %all-gather.5.cloned.1.call-done) | copy-start | bytes 22020100
  295.5 19.8 %copy-start.9 = (bf16[128,2,256]{2,0,1:T(8,128)(2,1)S(1)}, bf16[128,2,256]{2,0,1:T(8,128)(2,1)}, u32[]{:S(2)}) copy-start(bf16[128,2,256]{2,0,1:T(8,128)(2,1)} %copy-done.8) | copy-start | bytes 393220
  295.5 21.7 %copy-start.19 = (bf16[128,2,256]{2,0,1:T(8,128)(2,1)S(1)}, bf16[128,2,256]{2,0,1:T(8,128)(2,1)}, u32[]{:S(2)}) copy-start(bf16[128,2,256]{2,0,1:T(8,128)(2,1)} %copy-done.18) | copy-start | bytes 393220
  295.5 28.3 %copy-start.7 = (bf16[128,2,256]{2,0,1:T(8,128)(2,1)S(1)}, bf16[128,2,256]{2,0,1:T(8,128)(2,1)}, u32[]{:S(2)}) copy-start(bf16[128,2,256]{2,0,1:T(8,128)(2,1)} %copy-done.6) | copy-start | bytes 393220
  301.5 23.3 %copy-start.17 = (bf16[128,2,256]{2,0,1:T(8,128)(2,1)S(1)}, bf16[128,2,256]{2,0,1:T(8,128)(2,1)}, u32[]{:S(2)}) copy-start(bf16[128,2,256]{2,0,1:T(8,128)(2,1)} %copy-done.16) | copy-start | bytes 393220
  301.5 32.2 %copy-start.5 = (bf16[128,2,256]{2,0,1:T(8,128)(2,1)S(1)}, bf16[128,2,256]{2,0,1:T(8,128)(2,1)}, u32[]{:S(2)}) copy-start(bf16[128,2,256]{2,0,1:T(8,128)(2,1)} %copy-done.4) | copy-start | bytes 393220
  301.5 33.2 %copy-start.15 = (bf16[128,2,256]{2,0,1:T(8,128)(2,1)S(1)}, bf16[128,2,256]{2,0,1:T(8,128)(2,1)}, u32[]{:S(2)}) copy-start(bf16[128,2,256]{2,0,1:T(8,128)(2,1)} %copy-done.14) | copy-start | bytes 393220
  301.5 62.0 %all-gather.3.cloned.1.call-start = ((), (), s32[]{:S(2)}) async-start(), calls=%async_computation.5 | async-start | bytes 3899392 | tf_op jit(solution)/shard_map/all_gather | solution.py:69
  301.6 36.4 %copy-start.3 = (bf16[128,2,256]{0,2,1:T(8,128)(2,1)S(1)}, bf16[128,2,256]{0,2,1:T(8,128)(2,1)}, u32[]{:S(2)}) copy-start(bf16[128,2,256]{0,2,1:T(8,128)(2,1)} %copy-done.2) | copy-start | bytes 393220
  302.1 139.7 %all-reduce.3.cloned.1.call-start = ((), (), s32[]{:S(2)}) async-start(), calls=%async_computation.10 | async-start | bytes 5242880 | tf_op jit(solution)/shard_map/psum | solution.py:104
  312.9 26.0 %copy-start.13 = (bf16[128,2,256]{0,2,1:T(8,128)(2,1)S(1)}, bf16[128,2,256]{0,2,1:T(8,128)(2,1)}, u32[]{:S(2)}) copy-start(bf16[128,2,256]{0,2,1:T(8,128)(2,1)} %copy-done.12) | copy-start | bytes 393220
  312.9 9.0 %collective-permute-start.4 = (bf16[128,2,256]{2,0,1:T(8,128)(2,1)S(1)}, bf16[128,2,256]{2,0,1:T(8,128)(2,1)S(1)}, u32[]{:S(2)}, u32[]{:S(2)}) collective-permute-start(bf16[128,2,256]{2,0,1:T(8,128)(2,1)S(1)} %fusion.19), channel_id=1, source_target_pairs={{0,8},{8,0},{1,9},{9,1},{2,10},{10,2},{3,11},{11,3},{4,12},{12,4},... | collective-permute-start | bytes 393224 | tf_op jit(solution)/shard_map/ppermute | solution.py:17
  319.1 21.0 %copy-start.11 = (bf16[128,1,2,1,256]{0,4,2,3,1:T(8,128)(2,1)S(1)}, bf16[128,1,2,1,256]{0,4,2,3,1:T(8,128)(2,1)}, u32[]{:S(2)}) copy-start(bf16[128,1,2,1,256]{0,4,2,3,1:T(8,128)(2,1)} %copy-done.10) | copy-start | bytes 393220
  323.0 18.0 %copy-start.1 = (bf16[128,512]{0,1:T(8,128)(2,1)S(1)}, bf16[128,512]{0,1:T(8,128)(2,1)}, u32[]{:S(2)}) copy-start(bf16[128,512]{0,1:T(8,128)(2,1)} %copy-done) | copy-start | bytes 393220
  323.3 8.4 %collective-permute-start.5 = (bf16[128,2,256]{2,0,1:T(8,128)(2,1)S(1)}, bf16[128,2,256]{2,0,1:T(8,128)(2,1)S(1)}, u32[]{:S(2)}, u32[]{:S(2)}) collective-permute-start(bf16[128,2,256]{2,0,1:T(8,128)(2,1)S(1)} %fusion.20), channel_id=1, source_target_pairs={{0,4},{4,0},{1,5},{5,1},{2,6},{6,2},{3,7},{7,3},{8,12},{12,8},{9,1... | collective-permute-start | bytes 393224 | tf_op jit(solution)/shard_map/ppermute | solution.py:17
  332.2 5.3 %collective-permute-start.6 = (bf16[128,2,256]{2,0,1:T(8,128)(2,1)S(1)}, bf16[128,2,256]{2,0,1:T(8,128)(2,1)S(1)}, u32[]{:S(2)}, u32[]{:S(2)}) collective-permute-start(bf16[128,2,256]{2,0,1:T(8,128)(2,1)S(1)} %fusion.21), channel_id=1, source_target_pairs={{0,2},{2,0},{1,3},{3,1},{4,6},{6,4},{5,7},{7,5},{8,10},{10,8},{9,1... | collective-permute-start | bytes 393224 | tf_op jit(solution)/shard_map/ppermute | solution.py:17
  337.9 2.0 collective-permute-start.7
  342.0 114.4 %reduce-scatter.7.cloned.1.call-start = ((), (), s32[]{:S(2)}) async-start(), calls=%async_computation.6 | async-start | bytes 393216 | tf_op jit(solution)/shard_map/reduce_scatter | solution.py:73
  441.8 6.9 %copy-start.20 = (bf16[1,512,256]{2,1,0:T(8,128)(2,1)S(1)}, bf16[1,512,256]{2,1,0:T(8,128)(2,1)}, u32[]{:S(2)}) copy-start(bf16[1,512,256]{2,1,0:T(8,128)(2,1)} %get-tuple-element.11) | copy-start | bytes 786436
  441.8 6.9 %copy-start.21 = (bf16[1,512,256]{2,1,0:T(8,128)(2,1)S(1)}, bf16[1,512,256]{2,1,0:T(8,128)(2,1)}, u32[]{:S(2)}) copy-start(bf16[1,512,256]{2,1,0:T(8,128)(2,1)} %get-tuple-element.12) | copy-start | bytes 786436
  441.8 6.9 %copy-start.22 = (bf16[1,512,256]{2,1,0:T(8,128)(2,1)S(1)}, bf16[1,512,256]{2,1,0:T(8,128)(2,1)}, u32[]{:S(2)}) copy-start(bf16[1,512,256]{2,1,0:T(8,128)(2,1)} %get-tuple-element.17) | copy-start | bytes 786436
Sparse Core Ops, SparseCore 0:
  54.3 92.3 reduce-scatter.4
  150.5 68.2 reduce-scatter.8
  221.9 67.1 all-gather.4
  301.6 10.0 reduce-scatter.10
  313.9 49.5 all-gather.2
  366.8 74.9 all-reduce.2
  444.7 11.6 reduce-scatter.6
where the time goes:
time: 464 us; the launch traced here: 463 us
  waiting for transfers between devices  345 us (74%)
  matrix products  55 us (12%)
  between operations  14.5 us (3%)
  local copies, waits for them, and re-layouts  13.3 us (3%)
  starting transfers between devices  13.2 us (3%)
  blocking collectives  11.3 us (2%)
  other arithmetic  10.8 us (2%)
    reduce_scatter x1, waiting for transfers between devices, per_device(): lax.psum_scatter(products.astype(jnp.bfloat16), 'mp', scatter_dimension=1...  78.1 us
    reduce_scatter x1, waiting for transfers between devices, per_device(): lax.psum_scatter(hidden_terms.astype(jnp.bfloat16), 'mp', scatter_dimensi...  71.1 us
    psum x1, waiting for transfers between devices, per_device(): lax.psum(self_part.astype(jnp.bfloat16), 'dp').astype(jnp.float32)  69.9 us
    all_gather x1, waiting for transfers between devices, per_device(): segment = lax.all_gather(stacked, 'mp', axis=1, tiled=True)  67.3 us
    ppermute x8, waiting for transfers between devices, swapped(): return lax.ppermute(block, axis, route)  22.8 us
    all_gather x1, waiting for transfers between devices, per_device(): lax.all_gather(hidden, 'mp', axis=0, tiled=True)  21.5 us
    dot_general x3, matrix products, contract_last(): lax.dot_general(left_side, right_side, (((1,), (1,)), ((), ())), preferre...  20.1 us
    ppermute x8, starting transfers between devices, swapped(): return lax.ppermute(block, axis, route)  12.8 us
  transfers between devices with their start and end apart: 15, of which 14 were waited for; matrix products, arithmetic and copies ran while one was open for 9% of the time, Pallas kernels for 0%

commit v1 on v0

v1 whole, which is shorter than its diff:
```python
import jax
import jax.numpy as jnp
from jax import lax
from jax.sharding import PartitionSpec as P

BLOCK = 256
SECTIONS = 5


def swapped(block, axis, stride):
    count = lax.axis_size(axis)
    route = []
    for low in range(count):
        high = low | 1 << stride
        if high != low and high < count:
            route += [(low, high), (high, low)]
    return lax.ppermute(block, axis, route)


def gather_dp(block):
    if lax.axis_size("dp") == 2:
        return jnp.concatenate([block, swapped(block, "dp", 0)], axis=0)
    return lax.all_gather(block, "dp", axis=0, tiled=True)


def scatter_dp(total):
    if lax.axis_size("dp") == 2:
        rows = total.shape[0] // 2
        return (
            total[:rows] + swapped(total[rows:].astype(jnp.bfloat16), "dp", 0).astype(jnp.float32)
        ).astype(jnp.bfloat16)
    return lax.psum_scatter(total.astype(jnp.bfloat16), "dp", scatter_dimension=0, tiled=True)


def local_partner(blocks, degree):
    tok_rows, amount, breadth = blocks.shape
    distance = 2**degree
    folded = blocks.reshape(tok_rows, amount // (2 * distance), 2, distance, breadth)
    return jnp.flip(folded, 2).reshape(tok_rows, amount, breadth)


def contract_last(left_side, right_side):
    return lax.dot_general(
        left_side, right_side, (((1,), (1,)), ((), ())), preferred_element_type=jnp.float32
    )


def reduce_mp(partial):
    return lax.psum_scatter(
        partial.astype(jnp.bfloat16), "mp", scatter_dimension=0, tiled=True
    ).astype(jnp.float32)


def gather_mp(share):
    return lax.all_gather(share, "mp", axis=0, tiled=True)


def per_device(tokens, gate_weight, up_weight, down_weight, factor_self, factor_cross, cotangent):
    tok_rows, local_width = tokens.shape
    per_dev = local_width // BLOCK
    local_bits = per_dev.bit_length() - 1
    hidden_grad = reduce_mp(contract_last(gather_dp(cotangent), down_weight))
    current = tokens.reshape(tok_rows, per_dev, BLOCK)
    kept = []
    for degree in range(SECTIONS):
        self_mat = factor_self[degree].reshape(per_dev, BLOCK, BLOCK)
        cross_mat = factor_cross[degree].reshape(per_dev, BLOCK, BLOCK)
        if degree < local_bits:
            partner = local_partner(current, degree)
            kept += [current.reshape(tok_rows, local_width)]
        else:
            partner = swapped(current, "mp", degree - local_bits)
            kept += [current.reshape(tok_rows, local_width), partner.reshape(tok_rows, local_width)]
        result = jnp.einsum("tkb,kbc->tkc", current, self_mat, preferred_element_type=jnp.float32)
        result = result + jnp.einsum(
            "tkb,kbc->tkc", partner, cross_mat, preferred_element_type=jnp.float32
        )
        current = result.astype(jnp.bfloat16)
    rotated = current.reshape(tok_rows, local_width)
    segment = gather_dp(rotated)
    kept = gather_dp(jnp.concatenate(kept, axis=1))
    gate_sum = reduce_mp(jnp.dot(segment, gate_weight, preferred_element_type=jnp.float32))
    up_sum = reduce_mp(jnp.dot(segment, up_weight, preferred_element_type=jnp.float32))
    logistic = jax.nn.sigmoid(gate_sum)
    gate_grad = (hidden_grad * up_sum * logistic * (1.0 + gate_sum * (1.0 - logistic))).astype(
        jnp.bfloat16
    )
    up_grad = (hidden_grad * gate_sum * logistic).astype(jnp.bfloat16)
    hidden = (jax.nn.silu(gate_sum) * up_sum).astype(jnp.bfloat16)
    rot_terms = contract_last(gather_mp(gate_grad), gate_weight) + contract_last(
        gather_mp(up_grad), up_weight
    )
    gradient = scatter_dp(rot_terms)
    partial_value = jnp.dot(gather_mp(hidden), down_weight, preferred_element_type=jnp.float32)
    mixed_out = scatter_dp(partial_value)

    all_rows = kept.shape[0]
    kept = kept.reshape(all_rows, -1, per_dev, BLOCK)
    place = kept.shape[1]
    gradient = gradient.reshape(tok_rows, per_dev, BLOCK)
    self_list = [None] * SECTIONS
    cross_list = [None] * SECTIONS
    for degree in reversed(range(SECTIONS)):
        self_mat = factor_self[degree].reshape(per_dev, BLOCK, BLOCK)
        cross_mat = factor_cross[degree].reshape(per_dev, BLOCK, BLOCK)
        gathered = gather_dp(gradient)
        if degree < local_bits:
            place -= 1
            ours = kept[:, place]
            theirs = local_partner(ours, degree)
        else:
            place -= 2
            ours, theirs = kept[:, place], kept[:, place + 1]
        self_list[degree] = jnp.einsum(
            "tkb,tkc->kbc", ours, gathered, preferred_element_type=jnp.float32
        ).reshape(per_dev * BLOCK, BLOCK)
        cross_list[degree] = jnp.einsum(
            "tkb,tkc->kbc", theirs, gathered, preferred_element_type=jnp.float32
        ).reshape(per_dev * BLOCK, BLOCK)
        direct = jnp.einsum("tkc,kbc->tkb", gradient, self_mat, preferred_element_type=jnp.float32)
        carried = jnp.einsum(
            "tkc,kbc->tkb", gradient, cross_mat, preferred_element_type=jnp.float32
        )
        if degree < local_bits:
            returned = local_partner(carried, degree)
        else:
            returned = swapped(carried.astype(jnp.bfloat16), "mp", degree - local_bits).astype(
                carried.dtype
            )
        gradient = (direct + returned).astype(jnp.bfloat16)
    self_grad = jnp.stack(self_list)
    cross_grad = jnp.stack(cross_list)
    return (mixed_out, gradient.reshape(tok_rows, local_width), self_grad, cross_grad)


def solution(mesh):
    return jax.shard_map(
        per_device,
        mesh=mesh,
        in_specs=(
            P("dp", "mp"),
            P("mp", "dp"),
            P("mp", "dp"),
            P("dp", "mp"),
            P(None, "mp", None),
            P(None, "mp", None),
            P("dp", "mp"),
        ),
        out_specs=(P("dp", "mp"), P("dp", "mp"), P(None, "mp", None), P(None, "mp", None)),
        check_vma=False,
    )
```

time: 464 us -> 436 us (0.940)
  waiting for transfers between devices: 345 us -> 323 us
  blocking collectives: 11.3 us -> 0 us
  starting transfers between devices: 13.2 us -> 24.2 us
  other arithmetic: 10.8 us -> 5.51 us
    psum x1 -> x0, waiting for transfers between devices: 69.9 us -> none  [per_device(): lax.psum(self_part.astype(jnp.bfloat16), 'dp').astype(jnp.float32)]
    ppermute x8 -> x18, waiting for transfers between devices: 22.8 us -> 56.1 us  [swapped(): return lax.ppermute(block, axis, route)]
    all_gather x2 -> x0, blocking collectives: 11.3 us -> none  [the longest x1 5.67 us: per_device(): segment = lax.all_gather(rotated, 'dp', axis=0, tiled=True)]
    ppermute x8 -> x18, starting transfers between devices: 12.8 us -> 23.8 us  [swapped(): return lax.ppermute(block, axis, route)]
    another operation x5 -> x0, other arithmetic: 9.7 us -> none  [the longest x1 3.52 us: per_device(): jnp.stack([jnp.dot(segment, gate_weight, preferred_element_type=jnp.float...]
    all_gather x2 -> x3, waiting for transfers between devices: 88.8 us -> 95.9 us  [gather_mp(): return lax.all_gather(share, 'mp', axis=0, tiled=True)]
    reduce_scatter x4 -> x3, waiting for transfers between devices: 163 us -> 170 us  [reduce_mp(): lax.psum_scatter(partial.astype(jnp.bfloat16), 'mp', scatter_dimension=0,...]
  transfers between devices with their start and end apart: 15 -> 24, of which waited for: 14 -> 17; matrix products, arithmetic and copies ran while one was open for 9% -> 13% of each run, Pallas kernels for 0% -> 0%
where the time goes in v1:
time: 436 us
  waiting for transfers between devices  323 us (74%)
  matrix products  56.6 us (13%)
  starting transfers between devices  24.2 us (6%)
  between operations  14.8 us (3%)
  local copies, waits for them, and re-layouts  12.1 us (3%)
  other arithmetic  5.51 us (1%)
    reduce_scatter x3, waiting for transfers between devices, reduce_mp(): lax.psum_scatter(partial.astype(jnp.bfloat16), 'mp', scatter_dimension=0,...  170 us
    all_gather x3, waiting for transfers between devices, gather_mp(): return lax.all_gather(share, 'mp', axis=0, tiled=True)  95.9 us
    ppermute x18, waiting for transfers between devices, swapped(): return lax.ppermute(block, axis, route)  56.1 us
    ppermute x18, starting transfers between devices, swapped(): return lax.ppermute(block, axis, route)  23.8 us
    dot_general x3, matrix products, contract_last(): lax.dot_general(left_side, right_side, (((1,), (1,)), ((), ())), preferre...  20.6 us
  transfers between devices with their start and end apart: 24, of which 17 were waited for; matrix products, arithmetic and copies ran while one was open for 13% of the time, Pallas kernels for 0%

profile of v1, /device:TPU:0, one launch (start us, length us, event | category | flops | bytes accessed | tf_op | source)
XLA Modules:
  0.0 435.7 jit_solution(10609789485792911741)
XLA Ops:
  7.2 3.0 collective-permute-start.6
  10.2 3.7 collective-permute-done.6
  13.9 7.1 %convolution_convert_fusion = bf16[256,7168]{1,0:T(8,128)(2,1)} fusion(bf16[7168,512]{1,0:T(8,128)(2,1)} %param.10, bf16[128,512]{1,0:T(8,128)(2,1)S(1)} %collective-permute-done.6, bf16[128,512]{1,0:T(8,128)(2,1)} %param.13), kind=kOutput, calls=%fused_computation | convolution fusion | flops 1881407488 | bytes 11272192 | tf_op jit(solution)/shard_map/dot_general | solution.py:43
  22.8 1.4 fusion.66
  24.9 1.1 collective-permute-done
  26.2 1.8 collective-permute-start.1
  28.2 3.6 collective-permute-done.1
  32.1 1.9 collective-permute-start.2
  34.1 3.0 collective-permute-done.2
  37.3 2.9 collective-permute-start.3
  40.4 4.4 %collective-permute-done.3 = bf16[128,2,256]{2,0,1:T(8,128)(2,1)S(1)} collective-permute-done((bf16[128,2,256]{2,0,1:T(8,128)(2,1)S(1)}, bf16[128,2,256]{2,0,1:T(8,128)(2,1)S(1)}, u32[]{:S(2)}, u32[]{:S(2)}) %collective-permute-start.3) | collective-permute-done | bytes 131104 | tf_op jit(solution)/shard_map/ppermute | solution.py:17
  45.1 1.6 collective-permute-start.4
  46.7 3.4 collective-permute-done.4
  50.2 7.5 %convolution_convert_fusion.2 = bf16[256,7168]{1,0:T(8,128)(2,1)} fusion(bf16[512,7168]{1,0:T(8,128)(2,1)} %param.8, bf16[128,512]{0,1:T(8,128)(2,1)S(1)} %collective-permute-done.4, bf16[128,512]{0,1:T(8,128)(2,1)S(1)} %bitcast.238), kind=kOutput, calls=%fused_computation.2 | convolution fusion | flops 1881407488 | bytes 11272192 | tf_op jit(solution)/shard_map/dot_general | solution.py:82
  57.8 7.1 %convolution_convert_fusion.1 = bf16[256,7168]{1,0:T(8,128)(2,1)} fusion(bf16[512,7168]{1,0:T(8,128)(2,1)} %param.9, bf16[128,512]{0,1:T(8,128)(2,1)S(1)} %collective-permute-done.4, bf16[128,512]{0,1:T(8,128)(2,1)S(1)} %bitcast.239), kind=kOutput, calls=%fused_computation.1 | convolution fusion | flops 1881407488 | bytes 11272192 | tf_op jit(solution)/shard_map/dot_general | solution.py:83
  65.0 26.4 %reduce-scatter.8.cloned.1.call-done = bf16[16,7168]{1,0:T(8,128)(2,1)} async-done(((bf16[256,7168]{1,0:T(8,128)(2,1)}), bf16[16,7168]{1,0:T(8,128)(2,1)}) %reduce-scatter.8.cloned.1.call-update) | async-done | bytes 229392 | tf_op jit(solution)/shard_map/reduce_scatter | solution.py:49
  91.4 71.9 %reduce-scatter.4.cloned.1.call-done = bf16[16,7168]{1,0:T(8,128)(2,1)} async-done(((bf16[256,7168]{1,0:T(8,128)(2,1)}), bf16[16,7168]{1,0:T(8,128)(2,1)}) %reduce-scatter.4.cloned.1.call-update) | async-done | bytes 229392 | tf_op jit(solution)/shard_map/reduce_scatter | solution.py:49
  163.3 71.3 %reduce-scatter.6.cloned.1.call-done = bf16[16,7168]{1,0:T(8,128)(2,1)} async-done(((bf16[256,7168]{1,0:T(8,128)(2,1)}), bf16[16,7168]{1,0:T(8,128)(2,1)}) %reduce-scatter.6.cloned.1.call-update) | async-done | bytes 229392 | tf_op jit(solution)/shard_map/reduce_scatter | solution.py:49
  234.6 2.3 fusion.30
  239.2 1.4 collective-permute-start.12
  240.6 25.0 %collective-permute-done.12 = bf16[128,4608]{0,1:T(8,128)(2,1)S(1)} collective-permute-done((bf16[128,4608]{0,1:T(8,128)(2,1)S(1)}, bf16[128,4608]{0,1:T(8,128)(2,1)S(1)}, u32[]{:S(2)}, u32[]{:S(2)}) %collective-permute-start.12) | collective-permute-done | bytes 1179680 | tf_op jit(solution)/shard_map/ppermute | solution.py:17
  265.7 1.6 pad_maximum_fusion
  268.0 1.7 reverse.4
  269.7 13.7 %all-gather.6.cloned.1.call-done = bf16[256,7168]{1,0:T(8,128)(2,1)} async-done(((bf16[16,7168]{1,0:T(8,128)(2,1)}), bf16[256,7168]{1,0:T(8,128)(2,1)}) %all-gather.6.cloned.1.call-update) | async-done | bytes 3670032 | tf_op jit(solution)/shard_map/all_gather | solution.py:55
  283.4 7.1 %fusion.72 = f32[256,512]{1,0:T(8,128)} fusion(bf16[256,7168]{1,0:T(8,128)(2,1)} %all-gather.6.cloned.1.call-done, bf16[512,7168]{1,0:T(8,128)(2,1)} %param.8), kind=kOutput, calls=%fused_computation.138 | convolution fusion | flops 1879048192 | bytes 11534336 | tf_op jit(solution)/shard_map/dot_general | solution.py:43
  290.6 41.8 %all-gather.8.cloned.1.call-done = bf16[256,7168]{1,0:T(8,128)(2,1)} async-done(((bf16[16,7168]{1,0:T(8,128)(2,1)}), bf16[256,7168]{1,0:T(8,128)(2,1)}) %all-gather.8.cloned.1.call-update) | async-done | bytes 3670032 | tf_op jit(solution)/shard_map/all_gather | solution.py:55
  332.4 6.3 %convolution_add_fusion = f32[256,512]{1,0:T(8,128)S(1)} fusion(f32[256,512]{1,0:T(8,128)} %fusion.72, bf16[256,7168]{1,0:T(8,128)(2,1)} %all-gather.8.cloned.1.call-done, bf16[512,7168]{1,0:T(8,128)(2,1)} %param.9), kind=kOutput, calls=%fused_computation.4 | convolution fusion | flops 1879179264 | bytes 12058624 | tf_op jit(solution)/shard_map/dot_general | solution.py:43
  339.5 1.5 collective-permute-start.7
  341.0 40.3 %all-gather.4.cloned.1.call-done = bf16[256,7168]{1,0:T(8,128)(2,1)} async-done(((bf16[16,7168]{1,0:T(8,128)(2,1)}), bf16[256,7168]{1,0:T(8,128)(2,1)}) %all-gather.4.cloned.1.call-update) | async-done | bytes 3670032 | tf_op jit(solution)/shard_map/all_gather | solution.py:55
  381.4 6.3 %fusion.71 = f32[256,512]{1,0:T(8,128)S(1)} fusion(bf16[256,7168]{1,0:T(8,128)(2,1)} %all-gather.4.cloned.1.call-done, bf16[7168,512]{1,0:T(8,128)(2,1)} %param.10), kind=kOutput, calls=%fused_computation.137 | convolution fusion | flops 1879048192 | bytes 11534336 | tf_op jit(solution)/shard_map/dot_general | solution.py:94
  387.7 1.5 collective-permute-start.5
  390.5 2.4 collective-permute-start.8
  394.2 5.5 %collective-permute-done.8 = bf16[128,2,256]{2,0,1:T(8,128)(2,1)S(1)} collective-permute-done((bf16[128,2,256]{2,0,1:T(8,128)(2,1)S(1)}, bf16[128,2,256]{2,0,1:T(8,128)(2,1)S(1)}, u32[]{:S(2)}, u32[]{:S(2)}) %collective-permute-start.8) | collective-permute-done | bytes 131104 | tf_op jit(solution)/shard_map/ppermute | solution.py:17
  401.8 1.0 fusion.35
  402.9 2.9 collective-permute-done.9
  406.0 1.5 collective-permute-start.15
  408.4 1.0 fusion.32
  409.4 1.0 fusion.36
  410.4 2.4 collective-permute-done.10
  414.0 1.0 fusion.33
  415.0 1.1 fusion.37
  416.5 1.5 collective-permute-start.13
  419.2 1.1 fusion.34
  420.3 1.1 fusion.38
  421.5 1.1 collective-permute-done.13
  422.6 1.1 fusion.44
  423.7 1.2 fusion.46
  426.6 1.5 copy-done.24
  (139 shorter events, 18.5 us)
Async XLA Ops:
  7.2 84.2 %reduce-scatter.8.cloned.1.call-start = ((), (), s32[]{:S(2)}) async-start(), calls=%async_computation.6 | async-start | bytes 3899392 | tf_op jit(solution)/shard_map/reduce_scatter | solution.py:49
  7.2 6.7 %collective-permute-start.6 = (bf16[128,512]{1,0:T(8,128)(2,1)}, bf16[128,512]{1,0:T(8,128)(2,1)S(1)}, u32[]{:S(2)}, u32[]{:S(2)}) collective-permute-start(bf16[128,512]{1,0:T(8,128)(2,1)} %param.13), channel_id=1, source_target_pairs={{0,16},{16,0},{1,17},{17,1},{2,18},{18,2},{3,19},{19,3},{4,20},{20... | collective-permute-start | bytes 393224 | tf_op jit(solution)/shard_map/ppermute | solution.py:17
  21.1 1.4 copy-start.19
  21.1 142.2 %reduce-scatter.4.cloned.1.call-start = ((), (), s32[]{:S(2)}) async-start(), calls=%async_computation.3 | async-start | bytes 3899392 | tf_op jit(solution)/shard_map/reduce_scatter | solution.py:49
  22.5 3.7 copy-start.4
  22.5 5.5 %copy-start.6 = (bf16[1,512,256]{2,1,0:T(8,128)(2,1)}, bf16[1,512,256]{2,1,0:T(8,128)(2,1)S(1)}, u32[]{:S(2)}) copy-start(bf16[1,512,256]{2,1,0:T(8,128)(2,1)S(1)} %get-tuple-element.14) | copy-start | bytes 786436
  22.6 11.4 %copy-start.8 = (bf16[1,512,256]{2,1,0:T(8,128)(2,1)}, bf16[1,512,256]{2,1,0:T(8,128)(2,1)S(1)}, u32[]{:S(2)}) copy-start(bf16[1,512,256]{2,1,0:T(8,128)(2,1)S(1)} %get-tuple-element.17) | copy-start | bytes 786436
  22.6 17.6 %copy-start.10 = (bf16[1,512,256]{2,1,0:T(8,128)(2,1)}, bf16[1,512,256]{2,1,0:T(8,128)(2,1)S(1)}, u32[]{:S(2)}) copy-start(bf16[1,512,256]{2,1,0:T(8,128)(2,1)S(1)} %get-tuple-element.13) | copy-start | bytes 786436
  24.3 16.1 %copy-start = (bf16[1,512,256]{2,1,0:T(8,128)(2,1)}, bf16[1,512,256]{2,1,0:T(8,128)(2,1)S(1)}, u32[]{:S(2)}) copy-start(bf16[1,512,256]{2,1,0:T(8,128)(2,1)S(1)} %get-tuple-element.12) | copy-start | bytes 786436
  24.3 20.5 %copy-start.2 = (bf16[1,512,256]{2,1,0:T(8,128)(2,1)}, bf16[1,512,256]{2,1,0:T(8,128)(2,1)S(1)}, u32[]{:S(2)}) copy-start(bf16[1,512,256]{2,1,0:T(8,128)(2,1)S(1)} %get-tuple-element.8) | copy-start | bytes 786436
  24.6 1.4 collective-permute-start
  26.2 5.6 %collective-permute-start.1 = (bf16[128,2,256]{2,0,1:T(8,128)(2,1)S(1)}, bf16[128,2,256]{2,0,1:T(8,128)(2,1)S(1)}, u32[]{:S(2)}, u32[]{:S(2)}) collective-permute-start(bf16[128,2,256]{2,0,1:T(8,128)(2,1)S(1)} %fusion.20), channel_id=1, source_target_pairs={{0,2},{2,0},{1,3},{3,1},{4,6},{6,4},{5,7},{7,5},{8,10},{10,8},{9,1... | collective-permute-start | bytes 393224 | tf_op jit(solution)/shard_map/ppermute | solution.py:17
  32.1 5.0 %collective-permute-start.2 = (bf16[128,2,256]{2,0,1:T(8,128)(2,1)S(1)}, bf16[128,2,256]{2,0,1:T(8,128)(2,1)S(1)}, u32[]{:S(2)}, u32[]{:S(2)}) collective-permute-start(bf16[128,2,256]{2,0,1:T(8,128)(2,1)S(1)} %fusion.19), channel_id=1, source_target_pairs={{0,4},{4,0},{1,5},{5,1},{2,6},{6,2},{3,7},{7,3},{8,12},{12,8},{9,1... | collective-permute-start | bytes 393224 | tf_op jit(solution)/shard_map/ppermute | solution.py:17
  37.3 7.5 %collective-permute-start.3 = (bf16[128,2,256]{2,0,1:T(8,128)(2,1)S(1)}, bf16[128,2,256]{2,0,1:T(8,128)(2,1)S(1)}, u32[]{:S(2)}, u32[]{:S(2)}) collective-permute-start(bf16[128,2,256]{2,0,1:T(8,128)(2,1)S(1)} %fusion.18), channel_id=1, source_target_pairs={{0,8},{8,0},{1,9},{9,1},{2,10},{10,2},{3,11},{11,3},{4,12},{12,4},... | collective-permute-start | bytes 393224 | tf_op jit(solution)/shard_map/ppermute | solution.py:17
  45.1 5.0 %collective-permute-start.4 = (bf16[128,512]{0,1:T(8,128)(2,1)S(1)}, bf16[128,512]{0,1:T(8,128)(2,1)S(1)}, u32[]{:S(2)}, u32[]{:S(2)}) collective-permute-start(bf16[128,512]{0,1:T(8,128)(2,1)S(1)} %bitcast.237), channel_id=1, source_target_pairs={{0,16},{16,0},{1,17},{17,1},{2,18},{18,2},{3,19},{19,3},{4,20},{20... | collective-permute-start | bytes 393224 | tf_op jit(solution)/shard_map/ppermute | solution.py:17
  57.7 176.9 %reduce-scatter.6.cloned.1.call-start = ((), (), s32[]{:S(2)}) async-start(), calls=%async_computation.4 | async-start | bytes 3899392 | tf_op jit(solution)/shard_map/reduce_scatter | solution.py:49
  64.9 218.5 %all-gather.6.cloned.1.call-start = ((), (), s32[]{:S(2)}) async-start(), calls=%async_computation.7 | async-start | bytes 3899392 | tf_op jit(solution)/shard_map/all_gather | solution.py:55
  236.9 95.5 %all-gather.8.cloned.1.call-start = ((), (), s32[]{:S(2)}) async-start(), calls=%async_computation.8 | async-start | bytes 3899392 | tf_op jit(solution)/shard_map/all_gather | solution.py:55
  237.5 143.9 %all-gather.4.cloned.1.call-start = ((), (), s32[]{:S(2)}) async-start(), calls=%async_computation.5 | async-start | bytes 3899392 | tf_op jit(solution)/shard_map/all_gather | solution.py:55
  239.2 1.5 copy-start.18
  239.2 26.5 %collective-permute-start.12 = (bf16[128,4608]{0,1:T(8,128)(2,1)S(1)}, bf16[128,4608]{0,1:T(8,128)(2,1)S(1)}, u32[]{:S(2)}, u32[]{:S(2)}) collective-permute-start(bf16[128,4608]{0,1:T(8,128)(2,1)S(1)} %constant_dynamic-update-slice_fusion), channel_id=1, source_target_pairs={{0,16},{16,0},{1,17},{17,1},{2,18},{18,2},{3,19},{19,3},{4,20},{20... | collective-permute-start | bytes 3538952 | tf_op jit(solution)/shard_map/ppermute | solution.py:17
  339.5 49.8 %collective-permute-start.7 = (bf16[128,512]{1,0:T(8,128)(2,1)S(1)}, bf16[128,512]{1,0:T(8,128)(2,1)}, u32[]{:S(2)}, u32[]{:S(2)}) collective-permute-start(bf16[128,512]{1,0:T(8,128)(2,1)S(1)} %slice.145), channel_id=1, source_target_pairs={{0,16},{16,0},{1,17},{17,1},{2,18},{18,2},{3,19},{19,3},{4,20},{20... | collective-permute-start | bytes 393224 | tf_op jit(solution)/shard_map/ppermute | solution.py:17
  381.4 7.9 %copy-start.23 = (f32[256,512]{1,0:T(8,128)S(1)}, f32[256,512]{1,0:T(8,128)}, u32[]{:S(2)}) copy-start(f32[256,512]{1,0:T(8,128)} %copy-done.22) | copy-start | bytes 1572868
  381.4 8.9 %copy-start.3 = (bf16[1,512,256]{2,1,0:T(8,128)(2,1)S(1)}, bf16[1,512,256]{2,1,0:T(8,128)(2,1)}, u32[]{:S(2)}) copy-start(bf16[1,512,256]{2,1,0:T(8,128)(2,1)} %copy-done.2) | copy-start | bytes 786436
  381.4 18.3 %copy-start.11 = (bf16[1,512,256]{2,1,0:T(8,128)(2,1)S(1)}, bf16[1,512,256]{2,1,0:T(8,128)(2,1)}, u32[]{:S(2)}) copy-start(bf16[1,512,256]{2,1,0:T(8,128)(2,1)} %copy-done.10) | copy-start | bytes 786436
  387.7 12.8 %copy-start.1 = (bf16[1,512,256]{2,1,0:T(8,128)(2,1)S(1)}, bf16[1,512,256]{2,1,0:T(8,128)(2,1)}, u32[]{:S(2)}) copy-start(bf16[1,512,256]{2,1,0:T(8,128)(2,1)} %copy-done) | copy-start | bytes 786436
  387.7 5.7 %collective-permute-start.5 = (bf16[128,512]{1,0:T(8,128)(2,1)S(1)}, bf16[128,512]{1,0:T(8,128)(2,1)S(1)}, u32[]{:S(2)}, u32[]{:S(2)}) collective-permute-start(bf16[128,512]{1,0:T(8,128)(2,1)S(1)} %slice.146), channel_id=1, source_target_pairs={{0,16},{16,0},{1,17},{17,1},{2,18},{18,2},{3,19},{19,3},{4,20},{20... | collective-permute-start | bytes 393224 | tf_op jit(solution)/shard_map/ppermute | solution.py:17
  390.2 15.5 %copy-start.9 = (bf16[1,512,256]{2,1,0:T(8,128)(2,1)S(1)}, bf16[1,512,256]{2,1,0:T(8,128)(2,1)}, u32[]{:S(2)}) copy-start(bf16[1,512,256]{2,1,0:T(8,128)(2,1)} %copy-done.8) | copy-start | bytes 786436
  390.5 9.1 %collective-permute-start.8 = (bf16[128,2,256]{2,0,1:T(8,128)(2,1)S(1)}, bf16[128,2,256]{2,0,1:T(8,128)(2,1)S(1)}, u32[]{:S(2)}, u32[]{:S(2)}) collective-permute-start(bf16[128,2,256]{2,0,1:T(8,128)(2,1)S(1)} %fusion.13), channel_id=1, source_target_pairs={{0,8},{8,0},{1,9},{9,1},{2,10},{10,2},{3,11},{11,3},{4,12},{12,4},... | collective-permute-start | bytes 393224 | tf_op jit(solution)/shard_map/ppermute | solution.py:17
  392.9 7.9 %collective-permute-start.17 = (bf16[128,2,256]{2,0,1:T(8,128)(2,1)S(1)}, bf16[128,2,256]{2,0,1:T(8,128)(2,1)S(1)}, u32[]{:S(2)}, u32[]{:S(2)}) collective-permute-start(bf16[128,2,256]{2,0,1:T(8,128)(2,1)S(1)} %bitcast.251), channel_id=1, source_target_pairs={{0,16},{16,0},{1,17},{17,1},{2,18},{18,2},{3,19},{19,3},{4,20},{20... | collective-permute-start | bytes 393224 | tf_op jit(solution)/shard_map/ppermute | solution.py:17
  399.9 8.5 %collective-permute-start.16 = (bf16[128,2,256]{2,0,1:T(8,128)(2,1)S(1)}, bf16[128,2,256]{2,0,1:T(8,128)(2,1)S(1)}, u32[]{:S(2)}, u32[]{:S(2)}) collective-permute-start(bf16[128,2,256]{2,0,1:T(8,128)(2,1)S(1)} %add_convert_fusion), channel_id=1, source_target_pairs={{0,16},{16,0},{1,17},{17,1},{2,18},{18,2},{3,19},{19,3},{4,20},{20... | collective-permute-start | bytes 393224 | tf_op jit(solution)/shard_map/ppermute | solution.py:17
  400.7 5.0 %collective-permute-start.9 = (bf16[128,2,256]{2,0,1:T(8,128)(2,1)S(1)}, bf16[128,2,256]{2,0,1:T(8,128)(2,1)S(1)}, u32[]{:S(2)}, u32[]{:S(2)}) collective-permute-start(bf16[128,2,256]{2,0,1:T(8,128)(2,1)S(1)} %fusion.14), channel_id=1, source_target_pairs={{0,4},{4,0},{1,5},{5,1},{2,6},{6,2},{3,7},{7,3},{8,12},{12,8},{9,1... | collective-permute-start | bytes 393224 | tf_op jit(solution)/shard_map/ppermute | solution.py:17
  400.8 12.0 %copy-start.7 = (bf16[1,512,256]{2,1,0:T(8,128)(2,1)S(1)}, bf16[1,512,256]{2,1,0:T(8,128)(2,1)}, u32[]{:S(2)}) copy-start(bf16[1,512,256]{2,1,0:T(8,128)(2,1)} %copy-done.6) | copy-start | bytes 786436
  406.0 8.0 %collective-permute-start.15 = (bf16[128,2,256]{2,0,1:T(8,128)(2,1)S(1)}, bf16[128,2,256]{2,0,1:T(8,128)(2,1)S(1)}, u32[]{:S(2)}, u32[]{:S(2)}) collective-permute-start(bf16[128,2,256]{2,0,1:T(8,128)(2,1)S(1)} %fusion.9), channel_id=1, source_target_pairs={{0,16},{16,0},{1,17},{17,1},{2,18},{18,2},{3,19},{19,3},{4,20},{20... | collective-permute-start | bytes 393224 | tf_op jit(solution)/shard_map/ppermute | solution.py:17
  407.7 8.3 %copy-start.5 = (bf16[1,512,256]{2,1,0:T(8,128)(2,1)S(1)}, bf16[1,512,256]{2,1,0:T(8,128)(2,1)}, u32[]{:S(2)}) copy-start(bf16[1,512,256]{2,1,0:T(8,128)(2,1)} %copy-done.4) | copy-start | bytes 786436
  407.8 5.0 %collective-permute-start.10 = (bf16[128,2,256]{2,0,1:T(8,128)(2,1)S(1)}, bf16[128,2,256]{2,0,1:T(8,128)(2,1)S(1)}, u32[]{:S(2)}, u32[]{:S(2)}) collective-permute-start(bf16[128,2,256]{2,0,1:T(8,128)(2,1)S(1)} %fusion.15), channel_id=1, source_target_pairs={{0,2},{2,0},{1,3},{3,1},{4,6},{6,4},{5,7},{7,5},{8,10},{10,8},{9,1... | collective-permute-start | bytes 393224 | tf_op jit(solution)/shard_map/ppermute | solution.py:17
  413.0 6.2 %collective-permute-start.14 = (bf16[128,2,256]{2,0,1:T(8,128)(2,1)S(1)}, bf16[128,2,256]{2,0,1:T(8,128)(2,1)}, u32[]{:S(2)}, u32[]{:S(2)}) collective-permute-start(bf16[128,2,256]{2,0,1:T(8,128)(2,1)S(1)} %fusion.10), channel_id=1, source_target_pairs={{0,16},{16,0},{1,17},{17,1},{2,18},{18,2},{3,19},{19,3},{4,20},{20... | collective-permute-start | bytes 393224 | tf_op jit(solution)/shard_map/ppermute | solution.py:17
  413.9 2.2 collective-permute-start.11
  416.5 6.1 %collective-permute-start.13 = (bf16[128,2,256]{2,0,1:T(8,128)(2,1)S(1)}, bf16[128,2,256]{2,0,1:T(8,128)(2,1)}, u32[]{:S(2)}, u32[]{:S(2)}) collective-permute-start(bf16[128,2,256]{2,0,1:T(8,128)(2,1)S(1)} %fusion.11), channel_id=1, source_target_pairs={{0,16},{16,0},{1,17},{17,1},{2,18},{18,2},{3,19},{19,3},{4,20},{20... | collective-permute-start | bytes 393224 | tf_op jit(solution)/shard_map/ppermute | solution.py:17
  418.1 4.5 %copy-start.21 = (bf16[256,1,2,256]{0,3,2,1:T(8,128)(2,1)S(1)}, bf16[256,1,2,256]{0,3,2,1:T(8,128)(2,1)}, u32[]{:S(2)}) copy-start(bf16[256,1,2,256]{0,3,2,1:T(8,128)(2,1)} %reverse.4) | copy-start | bytes 786436
  421.5 3.6 copy-start.15
  423.7 1.4 copy-start.13
  424.9 1.0 copy-start.14
  425.0 1.2 copy-start.12
  425.0 1.3 copy-start.16
  425.1 1.4 copy-start.17
  426.5 1.5 copy-start.24
  426.6 2.3 copy-start.25
  (2 other events, 1.7 us)
Sparse Core Ops, SparseCore 0:
  21.2 70.1 reduce-scatter.7
  95.7 67.4 reduce-scatter.3
  167.1 67.4 reduce-scatter.5
  237.0 46.3 all-gather.5
  285.8 46.5 all-gather.7
  334.8 46.5 all-gather.3

commit v2 on v1

--- a/solution.py
+++ b/solution.py
@@ -1,6 +1,10 @@
+import functools
+
 import jax
 import jax.numpy as jnp
 from jax import lax
+from jax.experimental import pallas as pl
+from jax.experimental.pallas import tpu as pltpu
 from jax.sharding import PartitionSpec as P
 
 BLOCK = 256
@@ -45,21 +49,239 @@
     )
 
 
-def reduce_mp(partial):
-    return lax.psum_scatter(
-        partial.astype(jnp.bfloat16), "mp", scatter_dimension=0, tiled=True
-    ).astype(jnp.float32)
-
-
-def gather_mp(share):
-    return lax.all_gather(share, "mp", axis=0, tiled=True)
+def column_chunks(width):
+    for count in (4, 2):
+        if width % (count * 128) == 0:
+            return count, width // count
+    return 1, width
+
+
+def halves_of(me, stages, rows):
+    bits, starts, start = [], [], 0
+    for stage in range(stages):
+        bit = lax.rem(lax.div(me, 1 << stage), 2)
+        bits.append(bit)
+        starts.append(start)
+        start = start + bit * (rows >> (stage + 1))
+    starts.append(start)
+    return bits, starts
+
+
+def greet(partners):
+    barrier = pltpu.get_barrier_semaphore()
+    for partner in partners:
+        pl.semaphore_signal(
+            barrier, inc=1, device_id={"mp": partner}, device_id_type=pl.DeviceIdType.MESH
+        )
+    pl.semaphore_wait(barrier, len(partners))
+
+
+def reduce_kernel(stages, amount, turned, *refs):
+    left_ref, weights, outs = refs[0], refs[1 : 1 + amount], refs[1 + amount : 1 + 2 * amount]
+    weight_buf, part, *arrived, load_sem, send_sem, recv_sem = refs[1 + 2 * amount :]
+    rows = left_ref.shape[0]
+    width = outs[0].shape[1]
+    per_array, span = column_chunks(width)
+    chunks = [(array, piece) for array in range(amount) for piece in range(per_array)]
+    me = lax.axis_index("mp")
+
+    loads = []
+    for at, (array, piece) in enumerate(chunks):
+        cut = pl.ds(piece * span, span)
+        source = weights[array].at[cut, :] if turned else weights[array].at[:, cut]
+        loads.append(pltpu.make_async_copy(source, weight_buf.at[at], load_sem.at[at]))
+        loads[-1].start()
+
+    bits, _ = halves_of(me, stages, rows)
+    partners = [me + (1 - 2 * bits[stage]) * (1 << stage) for stage in range(stages)]
+    greet(partners)
+
+    copies = {}
+
+    def current(stage, at):
+        return part.at[at] if stage == 0 else arrived[stage - 1].at[at]
+
+    def send(stage, at):
+        half = rows >> (stage + 1)
+        first = pl.multiple_of((1 - bits[stage]) * half, half)
+        copies[stage, at] = pltpu.make_async_remote_copy(
+            src_ref=current(stage, at).at[pl.ds(first, half)],
+            dst_ref=arrived[stage].at[at],
+            send_sem=send_sem.at[stage, at],
+            recv_sem=recv_sem.at[stage, at],
+            device_id={"mp": partners[stage]},
+            device_id_type=pl.DeviceIdType.MESH,
+        )
+        copies[stage, at].start()
+
+    tile = 256 if span % 256 == 0 else 128 if span % 128 == 0 else span
+
+    def multiply(at):
+        loads[at].wait()
+
+        def one(step, _):
+            cut = pl.ds(pl.multiple_of(step * tile, tile), tile)
+            if turned:
+                product = contract_last(left_ref[...], weight_buf[at, cut, :])
+            else:
+                product = jnp.dot(
+                    left_ref[...], weight_buf[at, :, cut], preferred_element_type=jnp.float32
+                )
+            part[at, :, cut] = product.astype(jnp.bfloat16)
+            return 0
+
+        lax.fori_loop(0, span // tile, one, 0)
+
+    def receive(stage, at):
+        copies[stage, at].wait_recv()
+        half = rows >> (stage + 1)
+        step_rows = min(half, 16)
+        held = current(stage, at)
+        first = bits[stage] * half
+        array, piece = chunks[at]
+
+        def one(step, _):
+            here = pl.ds(pl.multiple_of(step * step_rows, step_rows), step_rows)
+            there = pl.ds(pl.multiple_of(first + step * step_rows, step_rows), step_rows)
+            total = arrived[stage][at, here, :].astype(jnp.float32) + held[there, :].astype(
+                jnp.float32
+            )
+            if stage == stages - 1:
+                outs[array][here, pl.ds(piece * span, span)] = total
+            else:
+                arrived[stage][at, here, :] = total.astype(jnp.bfloat16)
+            return 0
+
+        lax.fori_loop(0, half // step_rows, one, 0)
+        if stage < stages - 1:
+            send(stage + 1, at)
+
+    for turn in range(len(chunks) + stages):
+        if turn < len(chunks):
+            multiply(turn)
+            send(0, turn)
+        for stage in range(stages):
+            at = turn - 1 - stage
+            if 0 <= at < len(chunks):
+                receive(stage, at)
+    for copy in copies.values():
+        copy.wait_send()
+
+
+def reduce_mp(left, weights, turned, identity):
+    count = lax.axis_size("mp")
+    stages = count.bit_length() - 1
+    rows, depth = left.shape
+    width = weights[0].shape[0 if turned else 1]
+    amount = len(weights)
+    per_array, span = column_chunks(width)
+    chunks = amount * per_array
+    return pl.pallas_call(
+        functools.partial(reduce_kernel, stages, amount, turned),
+        out_shape=[jax.ShapeDtypeStruct((rows // count, width), jnp.float32)] * amount,
+        in_specs=[pl.BlockSpec(memory_space=pltpu.VMEM)]
+        + [pl.BlockSpec(memory_space=pl.ANY)] * amount,
+        out_specs=[pl.BlockSpec(memory_space=pltpu.VMEM)] * amount,
+        scratch_shapes=[
+            pltpu.VMEM((chunks, span, depth) if turned else (chunks, depth, span), jnp.bfloat16),
+            pltpu.VMEM((chunks, rows, span), jnp.bfloat16),
+        ]
+        + [
+            pltpu.VMEM((chunks, rows >> (stage + 1), span), jnp.bfloat16)
+            for stage in range(stages)
+        ]
+        + [
+            pltpu.SemaphoreType.DMA((chunks,)),
+            pltpu.SemaphoreType.DMA((stages, chunks)),
+            pltpu.SemaphoreType.DMA((stages, chunks)),
+        ],
+        compiler_params=pltpu.CompilerParams(
+            collective_id=identity, has_side_effects=True, vmem_limit_bytes=48 << 20
+        ),
+        cost_estimate=pl.CostEstimate(
+            flops=2 * rows * depth * width * amount,
+            bytes_accessed=amount * width * (depth + 20 * rows) * 2,
+            transcendentals=0,
+        ),
+    )(left, *weights)
+
+
+def gather_kernel(stages, amount, *refs):
+    shares, outs = refs[:amount], refs[amount : 2 * amount]
+    send_sem, recv_sem = refs[2 * amount :]
+    rows, width = outs[0].shape
+    per_array, span = column_chunks(width)
+    chunks = [(array, piece) for array in range(amount) for piece in range(per_array)]
+    me = lax.axis_index("mp")
+    bits, starts = halves_of(me, stages, rows)
+    partners = [me + (1 - 2 * bits[stage]) * (1 << stage) for stage in range(stages)]
+    least = rows >> stages
+    own = pl.ds(pl.multiple_of(starts[stages], least), least)
+    for array in range(amount):
+        outs[array][own, :] = shares[array][...]
+    greet(partners)
+
+    copies = {}
+
+    def send(stage, at):
+        array, piece = chunks[at]
+        size = rows >> (stage + 1)
+        region = outs[array].at[
+            pl.ds(pl.multiple_of(starts[stage + 1], size), size), pl.ds(piece * span, span)
+        ]
+        copies[stage, at] = pltpu.make_async_remote_copy(
+            src_ref=region,
+            dst_ref=region,
+            send_sem=send_sem.at[stage, at],
+            recv_sem=recv_sem.at[stage, at],
+            device_id={"mp": partners[stage]},
+            device_id_type=pl.DeviceIdType.MESH,
+        )
+        copies[stage, at].start()
+
+    for turn in range(len(chunks) + stages):
+        if turn < len(chunks):
+            send(stages - 1, turn)
+        for step in range(stages):
+            at = turn - 1 - step
+            stage = stages - 1 - step
+            if 0 <= at < len(chunks):
+                copies[stage, at].wait_recv()
+                if stage > 0:
+                    send(stage - 1, at)
+    for copy in copies.values():
+        copy.wait_send()
+
+
+def gather_mp(shares, identity):
+    count = lax.axis_size("mp")
+    stages = count.bit_length() - 1
+    rows, width = shares[0].shape
+    amount = len(shares)
+    chunks = amount * column_chunks(width)[0]
+    return pl.pallas_call(
+        functools.partial(gather_kernel, stages, amount),
+        out_shape=[jax.ShapeDtypeStruct((rows * count, width), jnp.bfloat16)] * amount,
+        in_specs=[pl.BlockSpec(memory_space=pltpu.VMEM)] * amount,
+        out_specs=[pl.BlockSpec(memory_space=pltpu.VMEM)] * amount,
+        scratch_shapes=[
+            pltpu.SemaphoreType.DMA((stages, chunks)),
+            pltpu.SemaphoreType.DMA((stages, chunks)),
+        ],
+        compiler_params=pltpu.CompilerParams(
+            collective_id=identity, has_side_effects=True, vmem_limit_bytes=48 << 20
+        ),
+        cost_estimate=pl.CostEstimate(
+            flops=0, bytes_accessed=amount * width * rows * count * 40, transcendentals=0
+        ),
+    )(*shares)
 
 
 def per_device(tokens, gate_weight, up_weight, down_weight, factor_self, factor_cross, cotangent):
     tok_rows, local_width = tokens.shape
     per_dev = local_width // BLOCK
     local_bits = per_dev.bit_length() - 1
-    hidden_grad = reduce_mp(contract_last(gather_dp(cotangent), down_weight))
+    (hidden_grad,) = reduce_mp(gather_dp(cotangent), [down_weight], True, 0)
     current = tokens.reshape(tok_rows, per_dev, BLOCK)
     kept = []
     for degree in range(SECTIONS):
@@ -79,19 +301,18 @@
     rotated = current.reshape(tok_rows, local_width)
     segment = gather_dp(rotated)
     kept = gather_dp(jnp.concatenate(kept, axis=1))
-    gate_sum = reduce_mp(jnp.dot(segment, gate_weight, preferred_element_type=jnp.float32))
-    up_sum = reduce_mp(jnp.dot(segment, up_weight, preferred_element_type=jnp.float32))
+    gate_sum, up_sum = reduce_mp(segment, [gate_weight, up_weight], False, 1)
     logistic = jax.nn.sigmoid(gate_sum)
     gate_grad = (hidden_grad * up_sum * logistic * (1.0 + gate_sum * (1.0 - logistic))).astype(
         jnp.bfloat16
     )
     up_grad = (hidden_grad * gate_sum * logistic).astype(jnp.bfloat16)
     hidden = (jax.nn.silu(gate_sum) * up_sum).astype(jnp.bfloat16)
-    rot_terms = contract_last(gather_mp(gate_grad), gate_weight) + contract_last(
-        gather_mp(up_grad), up_weight
-    )
+    gate_all, up_all = gather_mp([gate_grad, up_grad], 2)
+    rot_terms = contract_last(gate_all, gate_weight) + contract_last(up_all, up_weight)
     gradient = scatter_dp(rot_terms)
-    partial_value = jnp.dot(gather_mp(hidden), down_weight, preferred_element_type=jnp.float32)
+    (hidden_all,) = gather_mp([hidden], 3)
+    partial_value = jnp.dot(hidden_all, down_weight, preferred_element_type=jnp.float32)
     mixed_out = scatter_dp(partial_value)
 
     all_rows = kept.shape[0]

time: 436 us -> 278 us (0.64)
  waiting for transfers between devices: 323 us -> 24.1 us
  Pallas kernels: 0 us -> 181 us
  matrix products: 56.6 us -> 26.8 us
  between operations: 14.8 us -> 1.36 us
  local copies, waits for them, and re-layouts: 12.1 us -> 17.7 us
    pallas_call x0 -> x4, Pallas kernels: none -> 181 us  [the longest x2 93.4 us: reduce_mp(): pl.pallas_call(functools.partial(reduce_kernel, stages, amount, turned),...]
    reduce_scatter x3 -> x0, waiting for transfers between devices: 170 us -> none  [reduce_mp(): lax.psum_scatter(partial.astype(jnp.bfloat16), 'mp', scatter_dimension=0,...]
    all_gather x3 -> x0, waiting for transfers between devices: 95.9 us -> none  [gather_mp(): return lax.all_gather(share, 'mp', axis=0, tiled=True)]
    ppermute x18, waiting for transfers between devices: 56.1 us -> 24.1 us  [swapped(): return lax.ppermute(block, axis, route)]
    dot_general x3 -> x1, matrix products: 21 us -> 5.13 us  [per_device(): jnp.dot(hidden_all, down_weight, preferred_element_type=jnp.float32)]
    dot_general x3 -> x2, matrix products: 20.6 us -> 7.92 us  [contract_last(): lax.dot_general(left_side, right_side, (((1,), (1,)), ((), ())), preferre...]
    unnamed x71 -> x53, local copies, waits for them, and re-layouts: 6.98 us -> 11.3 us
  transfers between devices with their start and end apart: 24 -> 18, of which waited for: 17 -> 7; matrix products, arithmetic and copies ran while one was open for 13% -> 11% of each run, Pallas kernels for 0% -> 26%
where the time goes in v2:
time: 278 us
  Pallas kernels  181 us (65%)
  matrix products  26.8 us (10%)
  waiting for transfers between devices  24.1 us (9%)
  starting transfers between devices  20.6 us (7%)
  local copies, waits for them, and re-layouts  17.7 us (6%)
  other arithmetic  5.89 us (2%)
    pallas_call x2, Pallas kernels, reduce_mp(): pl.pallas_call(functools.partial(reduce_kernel, stages, amount, turned),...  93.4 us
    pallas_call x2, Pallas kernels, gather_mp(): pl.pallas_call(functools.partial(gather_kernel, stages, amount), out_shap...  88 us
    ppermute x18, waiting for transfers between devices, swapped(): return lax.ppermute(block, axis, route)  24.1 us
    ppermute x18, starting transfers between devices, swapped(): return lax.ppermute(block, axis, route)  20.6 us
    unnamed x53, local copies, waits for them, and re-layouts  11.3 us
    dot_general x2, matrix products, contract_last(): lax.dot_general(left_side, right_side, (((1,), (1,)), ((), ())), preferre...  7.92 us
  transfers between devices with their start and end apart: 18, of which 7 were waited for; matrix products, arithmetic and copies ran while one was open for 11% of the time, Pallas kernels for 26%

profile of v2, /device:TPU:0, one launch (start us, length us, event | category | flops | bytes accessed | tf_op | source)
XLA Modules:
  0.0 277.9 jit_solution(483110284910571346)
XLA Ops:
  0.7 3.0 %collective-permute-start.6 = (bf16[128,512]{1,0:T(8,128)(2,1)}, bf16[128,512]{1,0:T(8,128)(2,1)}, u32[]{:S(2)}, u32[]{:S(2)}) collective-permute-start(bf16[128,512]{1,0:T(8,128)(2,1)} %param.13), channel_id=1, source_target_pairs={{0,16},{16,0},{1,17},{17,1},{2,18},{18,2},{3,19},{19,3},{4,20},{20... | collective-permute-start | bytes 393224 | tf_op jit(solution)/shard_map/ppermute | solution.py:21
  3.7 1.4 fusion.51
  6.2 0.7 constant_dynamic-update-slice_fusion.8
  8.4 1.6 collective-permute-start.1
  10.0 0.9 fusion.52
  10.9 1.0 pad_maximum_fusion.2.refs_0_
  11.9 36.8 %shard_map.104 = f32[16,7168]{1,0:T(8,128)S(1)} custom-call(bf16[256,512]{1,0:T(8,128)(2,1)S(1)} %pad_maximum_fusion.2.refs_0_, bf16[7168,512]{1,0:T(8,128)(2,1)} %refs_1_.3), custom_call_target="tpu_custom_call" | custom-call | flops 1879048192 | bytes 80740352 | tf_op jit(solution)/shard_map/pallas_call | solution.py:179
  48.7 0.8 copy.35
  49.4 1.6 constant_dynamic-update-slice_fusion.6
  51.0 1.2 fusion.19
  52.2 1.6 collective-permute-start.2
  54.0 3.2 %collective-permute-done.2 = bf16[128,2,256]{2,0,1:T(8,128)(2,1)S(1)} collective-permute-done((bf16[128,2,256]{2,0,1:T(8,128)(2,1)S(1)}, bf16[128,2,256]{2,0,1:T(8,128)(2,1)S(1)}, u32[]{:S(2)}, u32[]{:S(2)}) %collective-permute-start.2) | collective-permute-done | bytes 131104 | tf_op jit(solution)/shard_map/ppermute | solution.py:21
  58.1 1.6 collective-permute-start.3
  59.9 5.5 %collective-permute-done.3 = bf16[128,2,256]{2,0,1:T(8,128)(2,1)S(1)} collective-permute-done((bf16[128,2,256]{2,0,1:T(8,128)(2,1)S(1)}, bf16[128,2,256]{2,0,1:T(8,128)(2,1)S(1)}, u32[]{:S(2)}, u32[]{:S(2)}) %collective-permute-start.3) | collective-permute-done | bytes 131104 | tf_op jit(solution)/shard_map/ppermute | solution.py:21
  67.1 1.0 copy.36
  68.1 0.7 constant_dynamic-update-slice_fusion.4
  68.8 2.0 collective-permute-done.4
  70.8 1.1 pad_maximum_fusion.1.refs_0_
  71.9 56.7 %shard_map.102 = (f32[16,7168]{1,0:T(8,128)S(1)}, f32[16,7168]{1,0:T(8,128)S(1)}) custom-call(bf16[256,512]{1,0:T(8,128)(2,1)S(1)} %pad_maximum_fusion.1.refs_0_, bf16[512,7168]{1,0:T(8,128)(2,1)} %refs_1_.2, bf16[512,7168]{1,0:T(8,128)(2,1)} %refs_2_.1), custom_call_target="tpu_custom_call" | custom-call | flops 3758096384 | bytes 161480704 | tf_op jit(solution)/shard_map/pallas_call | solution.py:179
  128.9 53.0 %shard_map.105 = (bf16[256,7168]{1,0:T(8,128)(2,1)S(1)}, bf16[256,7168]{1,0:T(8,128)(2,1)}) custom-call(bf16[16,7168]{1,0:T(8,128)(2,1)S(1)} %get-tuple-element.27.refs_0_, bf16[16,7168]{1,0:T(8,128)(2,1)S(1)} %get-tuple-element.26.refs_1_), custom_call_target="tpu_custom_call" | custom-call | bytes 146800640 | tf_op jit(solution)/shard_map/pallas_call | solution.py:262
  181.9 2.1 fusion.56
  184.0 5.8 %convolution_add_fusion = f32[256,512]{1,0:T(8,128)S(1)} fusion(f32[256,512]{1,0:T(8,128)S(1)} %fusion.56, bf16[256,7168]{1,0:T(8,128)(2,1)S(1)} %copy-done.14, bf16[512,7168]{1,0:T(8,128)(2,1)} %refs_2_.1), kind=kOutput, calls=%fused_computation.1 | convolution fusion | flops 1879179264 | bytes 12058624 | tf_op jit(solution)/shard_map/dot_general | solution.py:47
  191.6 0.7 constant_dynamic-update-slice_fusion.2
  192.3 3.6 %collective-permute-done.7 = bf16[128,512]{1,0:T(8,128)(2,1)S(1)} collective-permute-done((bf16[128,512]{1,0:T(8,128)(2,1)S(1)}, bf16[128,512]{1,0:T(8,128)(2,1)S(1)}, u32[]{:S(2)}, u32[]{:S(2)}) %collective-permute-start.7) | collective-permute-done | bytes 131104 | tf_op jit(solution)/shard_map/ppermute | solution.py:21
  195.8 1.0 fusion.29
  197.0 2.2 collective-permute-start.8
  199.8 1.0 copy.40
  200.9 0.7 constant_dynamic-update-slice_fusion
  202.1 35.0 %shard_map.103 = bf16[256,7168]{1,0:T(8,128)(2,1)S(1)} custom-call(bf16[16,7168]{1,0:T(8,128)(2,1)S(1)} %get-tuple-element.28.refs_0_), custom_call_target="tpu_custom_call" | custom-call | bytes 73400320 | tf_op jit(solution)/shard_map/pallas_call | solution.py:262
  237.6 2.3 collective-permute-start.9
  239.9 5.1 %fusion.55 = f32[256,512]{1,0:T(8,128)S(1)} fusion(bf16[256,7168]{1,0:T(8,128)(2,1)S(1)} %shard_map.103, bf16[7168,512]{1,0:T(8,128)(2,1)} %refs_1_.3), kind=kOutput, calls=%fused_computation.117 | convolution fusion | flops 1879048192 | bytes 11534336 | tf_op jit(solution)/shard_map/dot_general | solution.py:315
  245.1 2.1 collective-permute-start.17
  247.7 3.7 %collective-permute-done.5 = bf16[128,512]{1,0:T(8,128)(2,1)S(1)} collective-permute-done((bf16[128,512]{1,0:T(8,128)(2,1)S(1)}, bf16[128,512]{1,0:T(8,128)(2,1)S(1)}, u32[]{:S(2)}, u32[]{:S(2)}) %collective-permute-start.5) | collective-permute-done | bytes 131104 | tf_op jit(solution)/shard_map/ppermute | solution.py:21
  251.4 0.7 fusion.30
  253.7 1.8 collective-permute-start.15
  256.0 1.8 collective-permute-start.13
  258.4 0.8 copy.44
  259.2 1.9 pad_maximum_fusion
  261.1 0.7 reverse.4
  262.3 5.5 %collective-permute-done.13 = bf16[128,2,256]{2,0,1:T(8,128)(2,1)} collective-permute-done((bf16[128,2,256]{2,0,1:T(8,128)(2,1)S(1)}, bf16[128,2,256]{2,0,1:T(8,128)(2,1)}, u32[]{:S(2)}, u32[]{:S(2)}) %collective-permute-start.13) | collective-permute-done | bytes 131104 | tf_op jit(solution)/shard_map/ppermute | solution.py:21
  267.8 1.1 fusion.33
  268.9 1.1 fusion.31
  270.1 1.1 fusion.24
  271.3 1.1 fusion.23
  272.8 1.1 fusion.28
  274.0 1.1 fusion.27
  275.6 1.5 copy-done.12
  277.0 0.9 copy-done.13
  (107 shorter events, 13.9 us)
Async XLA Ops:
  0.6 4.4 %copy-start.2 = (bf16[5,512,256]{2,1,0:T(8,128)(2,1)S(1)}, bf16[5,512,256]{2,1,0:T(8,128)(2,1)}, u32[]{:S(2)}) copy-start(bf16[5,512,256]{2,1,0:T(8,128)(2,1)} %param.12) | copy-start | bytes 3932164
  0.6 4.5 %copy-start.3 = (bf16[128,512]{1,0:T(8,128)(2,1)S(1)}, bf16[128,512]{1,0:T(8,128)(2,1)}, u32[]{:S(2)}) copy-start(bf16[128,512]{1,0:T(8,128)(2,1)} %param.7) | copy-start | bytes 393220
  0.7 10.3 %collective-permute-start.6 = (bf16[128,512]{1,0:T(8,128)(2,1)}, bf16[128,512]{1,0:T(8,128)(2,1)}, u32[]{:S(2)}, u32[]{:S(2)}) collective-permute-start(bf16[128,512]{1,0:T(8,128)(2,1)} %param.13), channel_id=1, source_target_pairs={{0,16},{16,0},{1,17},{17,1},{2,18},{18,2},{3,19},{19,3},{4,20},{20... | collective-permute-start | bytes 393224 | tf_op jit(solution)/shard_map/ppermute | solution.py:21
  5.0 54.7 %copy-start = (bf16[1,512,256]{2,1,0:T(8,128)(2,1)}, bf16[1,512,256]{2,1,0:T(8,128)(2,1)S(1)}, u32[]{:S(2)}) copy-start(bf16[1,512,256]{2,1,0:T(8,128)(2,1)S(1)} %get-tuple-element.21) | copy-start | bytes 786436
  5.8 1.8 collective-permute-start
  7.5 0.7 copy-start.10
  8.4 42.6 %collective-permute-start.1 = (bf16[128,2,256]{2,0,1:T(8,128)(2,1)S(1)}, bf16[128,2,256]{2,0,1:T(8,128)(2,1)S(1)}, u32[]{:S(2)}, u32[]{:S(2)}) collective-permute-start(bf16[128,2,256]{2,0,1:T(8,128)(2,1)S(1)} %fusion.20), channel_id=1, source_target_pairs={{0,2},{2,0},{1,3},{3,1},{4,6},{6,4},{5,7},{7,5},{8,10},{10,8},{9,1... | collective-permute-start | bytes 393224 | tf_op jit(solution)/shard_map/ppermute | solution.py:21
  49.4 16.9 %copy-start.5 = (bf16[128,2,256]{0,2,1:T(8,128)(2,1)S(1)}, bf16[128,2,256]{0,2,1:T(8,128)(2,1)}, u32[]{:S(2)}) copy-start(bf16[128,2,256]{0,2,1:T(8,128)(2,1)} %copy.35) | copy-start | bytes 393220
  51.0 6.2 %copy-start.9 = (bf16[128,2,256]{2,0,1:T(8,128)(2,1)}, bf16[128,2,256]{2,0,1:T(8,128)(2,1)S(1)}, u32[]{:S(2)}) copy-start(bf16[128,2,256]{2,0,1:T(8,128)(2,1)S(1)} %collective-permute-done.1) | copy-start | bytes 393220
  52.2 5.0 %collective-permute-start.2 = (bf16[128,2,256]{2,0,1:T(8,128)(2,1)S(1)}, bf16[128,2,256]{2,0,1:T(8,128)(2,1)S(1)}, u32[]{:S(2)}, u32[]{:S(2)}) collective-permute-start(bf16[128,2,256]{2,0,1:T(8,128)(2,1)S(1)} %fusion.19), channel_id=1, source_target_pairs={{0,4},{4,0},{1,5},{5,1},{2,6},{6,2},{3,7},{7,3},{8,12},{12,8},{9,1... | collective-permute-start | bytes 393224 | tf_op jit(solution)/shard_map/ppermute | solution.py:21
  57.3 0.7 copy-start.7
  58.1 7.3 %collective-permute-start.3 = (bf16[128,2,256]{2,0,1:T(8,128)(2,1)S(1)}, bf16[128,2,256]{2,0,1:T(8,128)(2,1)S(1)}, u32[]{:S(2)}, u32[]{:S(2)}) collective-permute-start(bf16[128,2,256]{2,0,1:T(8,128)(2,1)S(1)} %fusion.18), channel_id=1, source_target_pairs={{0,8},{8,0},{1,9},{9,1},{2,10},{10,2},{3,11},{11,3},{4,12},{12,4},... | collective-permute-start | bytes 393224 | tf_op jit(solution)/shard_map/ppermute | solution.py:21
  65.4 0.8 copy-start.6
  65.7 5.1 %collective-permute-start.4 = (bf16[128,512]{1,0:T(8,128)(2,1)S(1)}, bf16[128,512]{1,0:T(8,128)(2,1)}, u32[]{:S(2)}, u32[]{:S(2)}) collective-permute-start(bf16[128,512]{1,0:T(8,128)(2,1)S(1)} %bitcast.248), channel_id=1, source_target_pairs={{0,16},{16,0},{1,17},{17,1},{2,18},{18,2},{3,19},{19,3},{4,20},{20... | collective-permute-start | bytes 393224 | tf_op jit(solution)/shard_map/ppermute | solution.py:21
  70.8 111.1 %slice-start = ((s8[7340032]{0:T(1024)(128)(4,1)}), s8[4194304]{0:T(1024)(128)(4,1)S(1)}, s32[]{:S(2)}) async-start(s8[7340032]{0:T(1024)(128)(4,1)} %bitcast.201), calls=%async_computation | async-start | bytes 8388608
  71.9 110.0 %slice-start.1 = ((s8[7340032]{0:T(1024)(128)(4,1)}), s8[3145728]{0:T(1024)(128)(4,1)S(1)}, s32[]{:S(2)}) async-start(s8[7340032]{0:T(1024)(128)(4,1)} %bitcast.201), calls=%async_computation.1 | async-start | bytes 6291456
  181.9 2.1 copy-start.14
  184.0 7.4 %copy-start.8 = (bf16[128,2,256]{2,0,1:T(8,128)(2,1)S(1)}, bf16[128,2,256]{2,0,1:T(8,128)(2,1)}, u32[]{:S(2)}) copy-start(bf16[128,2,256]{2,0,1:T(8,128)(2,1)} %copy-done.7) | copy-start | bytes 393220
  189.9 0.8 copy-start.11
  189.9 5.9 %collective-permute-start.7 = (bf16[128,512]{1,0:T(8,128)(2,1)S(1)}, bf16[128,512]{1,0:T(8,128)(2,1)S(1)}, u32[]{:S(2)}, u32[]{:S(2)}) collective-permute-start(bf16[128,512]{1,0:T(8,128)(2,1)S(1)} %slice.145), channel_id=1, source_target_pairs={{0,16},{16,0},{1,17},{17,1},{2,18},{18,2},{3,19},{19,3},{4,20},{20... | collective-permute-start | bytes 393224 | tf_op jit(solution)/shard_map/ppermute | solution.py:21
  196.8 40.4 %copy-start.1 = (bf16[1,512,256]{2,1,0:T(8,128)(2,1)S(1)}, bf16[1,512,256]{2,1,0:T(8,128)(2,1)}, u32[]{:S(2)}) copy-start(bf16[1,512,256]{2,1,0:T(8,128)(2,1)} %copy-done) | copy-start | bytes 786436
  197.0 40.1 %collective-permute-start.8 = (bf16[128,2,256]{2,0,1:T(8,128)(2,1)S(1)}, bf16[128,2,256]{2,0,1:T(8,128)(2,1)S(1)}, u32[]{:S(2)}, u32[]{:S(2)}) collective-permute-start(bf16[128,2,256]{2,0,1:T(8,128)(2,1)S(1)} %fusion.13), channel_id=1, source_target_pairs={{0,8},{8,0},{1,9},{9,1},{2,10},{10,2},{3,11},{11,3},{4,12},{12,4},... | collective-permute-start | bytes 393224 | tf_op jit(solution)/shard_map/ppermute | solution.py:21
  201.5 57.6 %collective-permute-start.12 = (bf16[128,4608]{0,1:T(8,128)(2,1)}, bf16[128,4608]{0,1:T(8,128)(2,1)}, u32[]{:S(2)}, u32[]{:S(2)}) collective-permute-start(bf16[128,4608]{0,1:T(8,128)(2,1)} %constant_dynamic-update-slice_fusion), channel_id=1, source_target_pairs={{0,16},{16,0},{1,17},{17,1},{2,18},{18,2},{3,19},{19,3},{4,20},{20... | collective-permute-start | bytes 3538952 | tf_op jit(solution)/shard_map/ppermute | solution.py:21
  237.6 9.6 %collective-permute-start.9 = (bf16[128,2,256]{2,0,1:T(8,128)(2,1)S(1)}, bf16[128,2,256]{2,0,1:T(8,128)(2,1)S(1)}, u32[]{:S(2)}, u32[]{:S(2)}) collective-permute-start(bf16[128,2,256]{2,0,1:T(8,128)(2,1)S(1)} %fusion.14), channel_id=1, source_target_pairs={{0,4},{4,0},{1,5},{5,1},{2,6},{6,2},{3,7},{7,3},{8,12},{12,8},{9,1... | collective-permute-start | bytes 393224 | tf_op jit(solution)/shard_map/ppermute | solution.py:21
  245.0 6.4 %collective-permute-start.5 = (bf16[128,512]{1,0:T(8,128)(2,1)S(1)}, bf16[128,512]{1,0:T(8,128)(2,1)S(1)}, u32[]{:S(2)}, u32[]{:S(2)}) collective-permute-start(bf16[128,512]{1,0:T(8,128)(2,1)S(1)} %slice.146), channel_id=1, source_target_pairs={{0,16},{16,0},{1,17},{17,1},{2,18},{18,2},{3,19},{19,3},{4,20},{20... | collective-permute-start | bytes 393224 | tf_op jit(solution)/shard_map/ppermute | solution.py:21
  245.1 8.5 %collective-permute-start.17 = (bf16[128,2,256]{2,0,1:T(8,128)(2,1)S(1)}, bf16[128,2,256]{2,0,1:T(8,128)(2,1)S(1)}, u32[]{:S(2)}, u32[]{:S(2)}) collective-permute-start(bf16[128,2,256]{2,0,1:T(8,128)(2,1)S(1)} %bitcast.250), channel_id=1, source_target_pairs={{0,16},{16,0},{1,17},{17,1},{2,18},{18,2},{3,19},{19,3},{4,20},{20... | collective-permute-start | bytes 393224 | tf_op jit(solution)/shard_map/ppermute | solution.py:21
  247.7 5.1 %collective-permute-start.10 = (bf16[128,2,256]{2,0,1:T(8,128)(2,1)S(1)}, bf16[128,2,256]{2,0,1:T(8,128)(2,1)S(1)}, u32[]{:S(2)}, u32[]{:S(2)}) collective-permute-start(bf16[128,2,256]{2,0,1:T(8,128)(2,1)S(1)} %fusion.15), channel_id=1, source_target_pairs={{0,2},{2,0},{1,3},{3,1},{4,6},{6,4},{5,7},{7,5},{8,10},{10,8},{9,1... | collective-permute-start | bytes 393224 | tf_op jit(solution)/shard_map/ppermute | solution.py:21
  253.2 2.6 collective-permute-start.11
  253.3 19.2 %collective-permute-start.16 = (bf16[128,2,256]{2,0,1:T(8,128)(2,1)S(1)}, bf16[128,2,256]{2,0,1:T(8,128)(2,1)S(1)}, u32[]{:S(2)}, u32[]{:S(2)}) collective-permute-start(bf16[128,2,256]{2,0,1:T(8,128)(2,1)S(1)} %add_convert_fusion), channel_id=1, source_target_pairs={{0,16},{16,0},{1,17},{17,1},{2,18},{18,2},{3,19},{19,3},{4,20},{20... | collective-permute-start | bytes 393224 | tf_op jit(solution)/shard_map/ppermute | solution.py:21
  253.7 17.6 %collective-permute-start.15 = (bf16[128,2,256]{2,0,1:T(8,128)(2,1)S(1)}, bf16[128,2,256]{2,0,1:T(8,128)(2,1)}, u32[]{:S(2)}, u32[]{:S(2)}) collective-permute-start(bf16[128,2,256]{2,0,1:T(8,128)(2,1)S(1)} %fusion.9), channel_id=1, source_target_pairs={{0,16},{16,0},{1,17},{17,1},{2,18},{18,2},{3,19},{19,3},{4,20},{20... | collective-permute-start | bytes 393224 | tf_op jit(solution)/shard_map/ppermute | solution.py:21
  255.5 14.6 %collective-permute-start.14 = (bf16[128,2,256]{2,0,1:T(8,128)(2,1)S(1)}, bf16[128,2,256]{2,0,1:T(8,128)(2,1)}, u32[]{:S(2)}, u32[]{:S(2)}) collective-permute-start(bf16[128,2,256]{2,0,1:T(8,128)(2,1)S(1)} %fusion.10), channel_id=1, source_target_pairs={{0,16},{16,0},{1,17},{17,1},{2,18},{18,2},{3,19},{19,3},{4,20},{20... | collective-permute-start | bytes 393224 | tf_op jit(solution)/shard_map/ppermute | solution.py:21
  256.0 11.8 %collective-permute-start.13 = (bf16[128,2,256]{2,0,1:T(8,128)(2,1)S(1)}, bf16[128,2,256]{2,0,1:T(8,128)(2,1)}, u32[]{:S(2)}, u32[]{:S(2)}) collective-permute-start(bf16[128,2,256]{2,0,1:T(8,128)(2,1)S(1)} %fusion.11), channel_id=1, source_target_pairs={{0,16},{16,0},{1,17},{17,1},{2,18},{18,2},{3,19},{19,3},{4,20},{20... | collective-permute-start | bytes 393224 | tf_op jit(solution)/shard_map/ppermute | solution.py:21
  261.8 7.1 %copy-start.4 = (bf16[256,1,2,256]{0,3,2,1:T(8,128)(2,1)S(1)}, bf16[256,1,2,256]{0,3,2,1:T(8,128)(2,1)}, u32[]{:S(2)}) copy-start(bf16[256,1,2,256]{0,3,2,1:T(8,128)(2,1)} %reverse.4) | copy-start | bytes 786436
  275.5 1.5 copy-start.12
  275.5 2.3 copy-start.13

commit v3 on v2

--- a/solution.py
+++ b/solution.py
@@ -76,20 +76,28 @@
     pl.semaphore_wait(barrier, len(partners))
 
 
-def reduce_kernel(stages, amount, turned, *refs):
-    left_ref, weights, outs = refs[0], refs[1 : 1 + amount], refs[1 + amount : 1 + 2 * amount]
-    weight_buf, part, *arrived, load_sem, send_sem, recv_sem = refs[1 + 2 * amount :]
-    rows = left_ref.shape[0]
+def reduce_kernel(stages, plan, lefts_held, *refs):
+    amount = len(plan)
+    lefts, refs = refs[:lefts_held], refs[lefts_held:]
+    weights, outs = refs[:amount], refs[amount : 2 * amount]
+    turned_buf, plain_buf, part, *arrived, load_sem, send_sem, recv_sem = refs[2 * amount :]
+    rows = lefts[0].shape[0]
     width = outs[0].shape[1]
     per_array, span = column_chunks(width)
     chunks = [(array, piece) for array in range(amount) for piece in range(per_array)]
     me = lax.axis_index("mp")
 
-    loads = []
+    loads, slots, used = [], [], [0, 0]
     for at, (array, piece) in enumerate(chunks):
         cut = pl.ds(piece * span, span)
-        source = weights[array].at[cut, :] if turned else weights[array].at[:, cut]
-        loads.append(pltpu.make_async_copy(source, weight_buf.at[at], load_sem.at[at]))
+        turned = plan[array][1]
+        slots.append(used[turned])
+        used[turned] += 1
+        if turned:
+            source, target = weights[array].at[cut, :], turned_buf.at[slots[at]]
+        else:
+            source, target = weights[array].at[:, cut], plain_buf.at[slots[at]]
+        loads.append(pltpu.make_async_copy(source, target, load_sem.at[at]))
         loads[-1].start()
 
     bits, _ = halves_of(me, stages, rows)
@@ -118,14 +126,16 @@
 
     def multiply(at):
         loads[at].wait()
+        left, turned = plan[chunks[at][0]]
+        left_ref, slot = lefts[left], slots[at]
 
         def one(step, _):
             cut = pl.ds(pl.multiple_of(step * tile, tile), tile)
             if turned:
-                product = contract_last(left_ref[...], weight_buf[at, cut, :])
+                product = contract_last(left_ref[...], turned_buf[slot, cut, :])
             else:
                 product = jnp.dot(
-                    left_ref[...], weight_buf[at, :, cut], preferred_element_type=jnp.float32
+                    left_ref[...], plain_buf[slot, :, cut], preferred_element_type=jnp.float32
                 )
             part[at, :, cut] = product.astype(jnp.bfloat16)
             return 0
@@ -168,22 +178,24 @@
         copy.wait_send()
 
 
-def reduce_mp(left, weights, turned, identity):
+def reduce_mp(lefts, weights, plan, identity):
     count = lax.axis_size("mp")
     stages = count.bit_length() - 1
-    rows, depth = left.shape
-    width = weights[0].shape[0 if turned else 1]
+    rows, depth = lefts[0].shape
+    width = weights[0].shape[0 if plan[0][1] else 1]
     amount = len(weights)
     per_array, span = column_chunks(width)
     chunks = amount * per_array
+    turned_chunks = per_array * sum(turned for _, turned in plan)
     return pl.pallas_call(
-        functools.partial(reduce_kernel, stages, amount, turned),
+        functools.partial(reduce_kernel, stages, plan, len(lefts)),
         out_shape=[jax.ShapeDtypeStruct((rows // count, width), jnp.float32)] * amount,
-        in_specs=[pl.BlockSpec(memory_space=pltpu.VMEM)]
+        in_specs=[pl.BlockSpec(memory_space=pltpu.VMEM)] * len(lefts)
         + [pl.BlockSpec(memory_space=pl.ANY)] * amount,
         out_specs=[pl.BlockSpec(memory_space=pltpu.VMEM)] * amount,
         scratch_shapes=[
-            pltpu.VMEM((chunks, span, depth) if turned else (chunks, depth, span), jnp.bfloat16),
+            pltpu.VMEM((turned_chunks, span, depth), jnp.bfloat16),
+            pltpu.VMEM((chunks - turned_chunks, depth, span), jnp.bfloat16),
             pltpu.VMEM((chunks, rows, span), jnp.bfloat16),
         ]
         + [
@@ -196,14 +208,14 @@
             pltpu.SemaphoreType.DMA((stages, chunks)),
         ],
         compiler_params=pltpu.CompilerParams(
-            collective_id=identity, has_side_effects=True, vmem_limit_bytes=48 << 20
+            collective_id=identity, has_side_effects=True, vmem_limit_bytes=56 << 20
         ),
         cost_estimate=pl.CostEstimate(
             flops=2 * rows * depth * width * amount,
             bytes_accessed=amount * width * (depth + 20 * rows) * 2,
             transcendentals=0,
         ),
-    )(left, *weights)
+    )(*lefts, *weights)
 
 
 def gather_kernel(stages, amount, *refs):
@@ -281,7 +293,7 @@
     tok_rows, local_width = tokens.shape
     per_dev = local_width // BLOCK
     local_bits = per_dev.bit_length() - 1
-    (hidden_grad,) = reduce_mp(gather_dp(cotangent), [down_weight], True, 0)
+    output_grad = gather_dp(cotangent)
     current = tokens.reshape(tok_rows, per_dev, BLOCK)
     kept = []
     for degree in range(SECTIONS):
@@ -301,17 +313,21 @@
     rotated = current.reshape(tok_rows, local_width)
     segment = gather_dp(rotated)
     kept = gather_dp(jnp.concatenate(kept, axis=1))
-    gate_sum, up_sum = reduce_mp(segment, [gate_weight, up_weight], False, 1)
+    hidden_grad, gate_sum, up_sum = reduce_mp(
+        [output_grad, segment],
+        [down_weight, gate_weight, up_weight],
+        ((0, True), (1, False), (1, False)),
+        0,
+    )
     logistic = jax.nn.sigmoid(gate_sum)
     gate_grad = (hidden_grad * up_sum * logistic * (1.0 + gate_sum * (1.0 - logistic))).astype(
         jnp.bfloat16
     )
     up_grad = (hidden_grad * gate_sum * logistic).astype(jnp.bfloat16)
     hidden = (jax.nn.silu(gate_sum) * up_sum).astype(jnp.bfloat16)
-    gate_all, up_all = gather_mp([gate_grad, up_grad], 2)
+    gate_all, up_all, hidden_all = gather_mp([gate_grad, up_grad, hidden], 1)
     rot_terms = contract_last(gate_all, gate_weight) + contract_last(up_all, up_weight)
     gradient = scatter_dp(rot_terms)
-    (hidden_all,) = gather_mp([hidden], 3)
     partial_value = jnp.dot(hidden_all, down_weight, preferred_element_type=jnp.float32)
     mixed_out = scatter_dp(partial_value)
 

time: 278 us -> 265 us (0.953)
  Pallas kernels: 181 us -> 154 us
  waiting for transfers between devices: 24.1 us -> 40.8 us
  local copies, waits for them, and re-layouts: 17.7 us -> 13.5 us
    ppermute x18, waiting for transfers between devices: 24.1 us -> 40.8 us  [swapped(): return lax.ppermute(block, axis, route)]
    pallas_call x2 -> x1, Pallas kernels: 88 us -> 74.1 us  [gather_mp(): pl.pallas_call(functools.partial(gather_kernel, stages, amount), out_shap...]
    pallas_call x2 -> x1, Pallas kernels: 93.4 us -> 80.3 us  [reduce_mp(): pl.pallas_call(functools.partial(reduce_kernel, stages, plan, len(lefts))...]
    unnamed x53 -> x79, local copies, waits for them, and re-layouts: 11.3 us -> 8.99 us
  transfers between devices with their start and end apart: 18 -> 18, of which waited for: 7 -> 8; matrix products, arithmetic and copies ran while one was open for 11% -> 11% of each run, Pallas kernels for 26% -> 0%
where the time goes in v3:
time: 265 us; the launch traced here: 264 us
  Pallas kernels  154 us (58%)
  waiting for transfers between devices  40.8 us (15%)
  matrix products  25.6 us (10%)
  starting transfers between devices  21.8 us (8%)
  local copies, waits for them, and re-layouts  13.5 us (5%)
  other arithmetic  6.52 us (2%)
    pallas_call x1, Pallas kernels, reduce_mp(): pl.pallas_call(functools.partial(reduce_kernel, stages, plan, len(lefts))...  80.3 us
    pallas_call x1, Pallas kernels, gather_mp(): pl.pallas_call(functools.partial(gather_kernel, stages, amount), out_shap...  74.1 us
    ppermute x18, waiting for transfers between devices, swapped(): return lax.ppermute(block, axis, route)  40.8 us
    ppermute x18, starting transfers between devices, swapped(): return lax.ppermute(block, axis, route)  21.8 us
    unnamed x79, local copies, waits for them, and re-layouts  8.99 us
    dot_general x2, matrix products, contract_last(): lax.dot_general(left_side, right_side, (((1,), (1,)), ((), ())), preferre...  7.32 us
    dot_general x1, matrix products, per_device(): jnp.dot(hidden_all, down_weight, preferred_element_type=jnp.float32)  6.29 us
  transfers between devices with their start and end apart: 18, of which 8 were waited for; matrix products, arithmetic and copies ran while one was open for 11% of the time, Pallas kernels for 0%

profile of v3, /device:TPU:0, one launch (start us, length us, event | category | flops | bytes accessed | tf_op | source)
XLA Modules:
  0.0 264.1 jit_solution(10677014481805832766)
XLA Ops:
  0.7 3.0 %collective-permute-start = (bf16[128,512]{1,0:T(8,128)(2,1)}, bf16[128,512]{1,0:T(8,128)(2,1)}, u32[]{:S(2)}, u32[]{:S(2)}) collective-permute-start(bf16[128,512]{1,0:T(8,128)(2,1)} %param.13), channel_id=1, source_target_pairs={{0,16},{16,0},{1,17},{17,1},{2,18},{18,2},{3,19},{19,3},{4,20},{20... | collective-permute-start | bytes 393224 | tf_op jit(solution)/shard_map/ppermute | solution.py:21
  3.7 1.4 fusion.51
  6.3 0.7 constant_dynamic-update-slice_fusion.8
  7.0 0.7 constant_dynamic-update-slice_fusion.7
  7.9 1.6 collective-permute-start.2
  9.6 0.7 constant_dynamic-update-slice_fusion.6
  10.5 1.6 pad_maximum_fusion.1.refs_0_
  12.1 1.7 collective-permute-done.2
  14.0 1.6 collective-permute-start.3
  15.9 3.3 %collective-permute-done.3 = bf16[128,2,256]{2,0,1:T(8,128)(2,1)S(1)} collective-permute-done((bf16[128,2,256]{2,0,1:T(8,128)(2,1)S(1)}, bf16[128,2,256]{2,0,1:T(8,128)(2,1)S(1)}, u32[]{:S(2)}, u32[]{:S(2)}) %collective-permute-start.3) | collective-permute-done | bytes 131104 | tf_op jit(solution)/shard_map/ppermute | solution.py:21
  19.4 2.7 %collective-permute-start.4 = (bf16[128,2,256]{2,0,1:T(8,128)(2,1)S(1)}, bf16[128,2,256]{2,0,1:T(8,128)(2,1)S(1)}, u32[]{:S(2)}, u32[]{:S(2)}) collective-permute-start(bf16[128,2,256]{2,0,1:T(8,128)(2,1)S(1)} %fusion.18), channel_id=1, source_target_pairs={{0,8},{8,0},{1,9},{9,1},{2,10},{10,2},{3,11},{11,3},{4,12},{12,4},... | collective-permute-start | bytes 393224 | tf_op jit(solution)/shard_map/ppermute | solution.py:21
  22.3 5.2 %collective-permute-done.4 = bf16[128,2,256]{2,0,1:T(8,128)(2,1)S(1)} collective-permute-done((bf16[128,2,256]{2,0,1:T(8,128)(2,1)S(1)}, bf16[128,2,256]{2,0,1:T(8,128)(2,1)S(1)}, u32[]{:S(2)}, u32[]{:S(2)}) %collective-permute-start.4) | collective-permute-done | bytes 131104 | tf_op jit(solution)/shard_map/ppermute | solution.py:21
  28.2 0.7 constant_dynamic-update-slice_fusion.5
  28.9 0.8 copy.37
  29.8 0.7 constant_dynamic-update-slice_fusion.4
  30.4 2.2 collective-permute-done.5
  32.7 0.7 pad_maximum_fusion.2.refs_1_
  33.4 80.3 %shard_map.102 = (f32[16,7168]{1,0:T(8,128)}, f32[16,7168]{1,0:T(8,128)}, f32[16,7168]{1,0:T(8,128)}) custom-call(bf16[256,512]{1,0:T(8,128)(2,1)} %pad_maximum_fusion.1.refs_0_, bf16[256,512]{1,0:T(8,128)(2,1)} %pad_maximum_fusion.2.refs_1_, bf16[7168,512]{1,0:T(8,128)(2,1)} %refs_2_.1, bf16[512,7168]{1,0:T(8,128)(2,1)} %refs_3_.1, bf16[512,7168]{1,0:T(8,128)(2,1)} %refs_4_.1), custom_call_target="tpu_custom_call" | custom-call | flops 5637144576 | bytes 242221056 | tf_op jit(solution)/shard_map/pallas_call | solution.py:190
  113.7 1.5 multiply_convert_fusion
  115.3 74.1 %shard_map.103 = (bf16[256,7168]{1,0:T(8,128)(2,1)S(1)}, bf16[256,7168]{1,0:T(8,128)(2,1)}, bf16[256,7168]{1,0:T(8,128)(2,1)}) custom-call(bf16[16,7168]{1,0:T(8,128)(2,1)S(1)} %get-tuple-element.31.refs_0_, bf16[16,7168]{1,0:T(8,128)(2,1)S(1)} %get-tuple-element.32.refs_1_, bf16[16,7168]{1,0:T(8,128)(2,1)S(1)} %get-tuple-element.30.refs_2_), custom_call_target="tpu_custom_call" | custom-call | bytes 220200960 | tf_op jit(solution)/shard_map/pallas_call | solution.py:274
  189.4 2.1 fusion.56
  191.6 5.2 %convolution_add_fusion = f32[256,512]{1,0:T(8,128)S(1)} fusion(f32[256,512]{1,0:T(8,128)S(1)} %fusion.56, bf16[256,7168]{1,0:T(8,128)(2,1)S(1)} %copy-done.27, bf16[512,7168]{1,0:T(8,128)(2,1)} %refs_4_.1), kind=kOutput, calls=%fused_computation.1 | convolution fusion | flops 1879179264 | bytes 12058624 | tf_op jit(solution)/shard_map/dot_general | solution.py:47
  197.4 0.7 constant_dynamic-update-slice_fusion.3
  198.3 0.7 constant_dynamic-update-slice_fusion.2
  199.0 3.8 %collective-permute-done.7 = bf16[128,512]{1,0:T(8,128)(2,1)S(1)} collective-permute-done((bf16[128,512]{1,0:T(8,128)(2,1)S(1)}, bf16[128,512]{1,0:T(8,128)(2,1)S(1)}, u32[]{:S(2)}, u32[]{:S(2)}) %collective-permute-start.7) | collective-permute-done | bytes 131104 | tf_op jit(solution)/shard_map/ppermute | solution.py:21
  203.0 2.1 collective-permute-start.8
  205.1 0.7 constant_dynamic-update-slice_fusion.1
  205.9 0.7 constant_dynamic-update-slice_fusion
  207.1 4.8 %collective-permute-done.8 = bf16[128,2,256]{2,0,1:T(8,128)(2,1)S(1)} collective-permute-done((bf16[128,2,256]{2,0,1:T(8,128)(2,1)S(1)}, bf16[128,2,256]{2,0,1:T(8,128)(2,1)S(1)}, u32[]{:S(2)}, u32[]{:S(2)}) %collective-permute-start.8) | collective-permute-done | bytes 131104 | tf_op jit(solution)/shard_map/ppermute | solution.py:21
  212.5 6.3 %fusion.55 = f32[256,512]{1,0:T(8,128)S(1)} fusion(bf16[256,7168]{1,0:T(8,128)(2,1)} %get-tuple-element.13, bf16[7168,512]{1,0:T(8,128)(2,1)} %refs_2_.1), kind=kOutput, calls=%fused_computation.117 | convolution fusion | flops 1879048192 | bytes 11534336 | tf_op jit(solution)/shard_map/dot_general | solution.py:331
  219.5 1.6 collective-permute-start.17
  221.5 2.4 collective-permute-start.10
  224.0 14.3 %collective-permute-done.6 = bf16[128,512]{1,0:T(8,128)(2,1)S(1)} collective-permute-done((bf16[128,512]{1,0:T(8,128)(2,1)S(1)}, bf16[128,512]{1,0:T(8,128)(2,1)S(1)}, u32[]{:S(2)}, u32[]{:S(2)}) %collective-permute-start.6) | collective-permute-done | bytes 131104 | tf_op jit(solution)/shard_map/ppermute | solution.py:21
  238.3 0.7 fusion.30
  240.1 1.6 collective-permute-start.15
  242.5 1.6 collective-permute-start.13
  244.7 0.8 copy.44
  245.4 1.9 pad_maximum_fusion
  247.4 0.7 reverse.4
  248.6 5.4 %collective-permute-done.13 = bf16[128,2,256]{2,0,1:T(8,128)(2,1)} collective-permute-done((bf16[128,2,256]{2,0,1:T(8,128)(2,1)S(1)}, bf16[128,2,256]{2,0,1:T(8,128)(2,1)}, u32[]{:S(2)}, u32[]{:S(2)}) %collective-permute-start.13) | collective-permute-done | bytes 131104 | tf_op jit(solution)/shard_map/ppermute | solution.py:21
  254.0 1.1 fusion.33
  255.2 1.1 fusion.31
  256.3 1.1 fusion.24
  257.6 1.1 fusion.23
  259.1 1.1 fusion.28
  260.3 1.1 fusion.27
  261.8 1.5 copy-done.25
  263.3 0.9 copy-done.26
  (131 shorter events, 10.5 us)
Async XLA Ops:
  0.6 4.4 %copy-start.16 = (bf16[5,512,256]{2,1,0:T(8,128)(2,1)S(1)}, bf16[5,512,256]{2,1,0:T(8,128)(2,1)}, u32[]{:S(2)}) copy-start(bf16[5,512,256]{2,1,0:T(8,128)(2,1)} %param.12) | copy-start | bytes 3932164
  0.6 4.5 %copy-start.17 = (bf16[128,512]{1,0:T(8,128)(2,1)S(1)}, bf16[128,512]{1,0:T(8,128)(2,1)}, u32[]{:S(2)}) copy-start(bf16[128,512]{1,0:T(8,128)(2,1)} %param.7) | copy-start | bytes 393220
  0.7 9.8 %collective-permute-start = (bf16[128,512]{1,0:T(8,128)(2,1)}, bf16[128,512]{1,0:T(8,128)(2,1)}, u32[]{:S(2)}, u32[]{:S(2)}) collective-permute-start(bf16[128,512]{1,0:T(8,128)(2,1)} %param.13), channel_id=1, source_target_pairs={{0,16},{16,0},{1,17},{17,1},{2,18},{18,2},{3,19},{19,3},{4,20},{20... | collective-permute-start | bytes 393224 | tf_op jit(solution)/shard_map/ppermute | solution.py:21
  5.0 1.3 copy-start.6
  5.0 4.4 %copy-start.8 = (bf16[1,512,256]{2,1,0:T(8,128)(2,1)}, bf16[1,512,256]{2,1,0:T(8,128)(2,1)S(1)}, u32[]{:S(2)}) copy-start(bf16[1,512,256]{2,1,0:T(8,128)(2,1)S(1)} %get-tuple-element.26) | copy-start | bytes 786436
  5.0 10.6 %copy-start.10 = (bf16[1,512,256]{2,1,0:T(8,128)(2,1)}, bf16[1,512,256]{2,1,0:T(8,128)(2,1)S(1)}, u32[]{:S(2)}) copy-start(bf16[1,512,256]{2,1,0:T(8,128)(2,1)S(1)} %get-tuple-element.29) | copy-start | bytes 786436
  5.0 17.0 %copy-start.12 = (bf16[1,512,256]{2,1,0:T(8,128)(2,1)}, bf16[1,512,256]{2,1,0:T(8,128)(2,1)S(1)}, u32[]{:S(2)}) copy-start(bf16[1,512,256]{2,1,0:T(8,128)(2,1)S(1)} %get-tuple-element.25) | copy-start | bytes 786436
  5.2 5.1 %copy-start = (bf16[1,512,256]{2,1,0:T(8,128)(2,1)}, bf16[1,512,256]{2,1,0:T(8,128)(2,1)S(1)}, u32[]{:S(2)}) copy-start(bf16[1,512,256]{2,1,0:T(8,128)(2,1)S(1)} %get-tuple-element.22) | copy-start | bytes 786436
  5.2 14.0 %copy-start.2 = (bf16[1,512,256]{2,1,0:T(8,128)(2,1)}, bf16[1,512,256]{2,1,0:T(8,128)(2,1)S(1)}, u32[]{:S(2)}) copy-start(bf16[1,512,256]{2,1,0:T(8,128)(2,1)S(1)} %get-tuple-element.24) | copy-start | bytes 786436
  5.2 22.2 %copy-start.4 = (bf16[1,512,256]{2,1,0:T(8,128)(2,1)}, bf16[1,512,256]{2,1,0:T(8,128)(2,1)S(1)}, u32[]{:S(2)}) copy-start(bf16[1,512,256]{2,1,0:T(8,128)(2,1)S(1)} %get-tuple-element.20) | copy-start | bytes 786436
  5.3 5.2 %copy-start.24 = (bf16[128,512]{1,0:T(8,128)(2,1)S(1)}, bf16[128,512]{1,0:T(8,128)(2,1)}, u32[]{:S(2)}) copy-start(bf16[128,512]{1,0:T(8,128)(2,1)} %param.13) | copy-start | bytes 393220
  5.8 1.8 collective-permute-start.1
  7.9 6.0 %collective-permute-start.2 = (bf16[128,2,256]{2,0,1:T(8,128)(2,1)S(1)}, bf16[128,2,256]{2,0,1:T(8,128)(2,1)S(1)}, u32[]{:S(2)}, u32[]{:S(2)}) collective-permute-start(bf16[128,2,256]{2,0,1:T(8,128)(2,1)S(1)} %fusion.20), channel_id=1, source_target_pairs={{0,2},{2,0},{1,3},{3,1},{4,6},{6,4},{5,7},{7,5},{8,10},{10,8},{9,1... | collective-permute-start | bytes 393224 | tf_op jit(solution)/shard_map/ppermute | solution.py:21
  14.0 5.2 %collective-permute-start.3 = (bf16[128,2,256]{2,0,1:T(8,128)(2,1)S(1)}, bf16[128,2,256]{2,0,1:T(8,128)(2,1)S(1)}, u32[]{:S(2)}, u32[]{:S(2)}) collective-permute-start(bf16[128,2,256]{2,0,1:T(8,128)(2,1)S(1)} %fusion.19), channel_id=1, source_target_pairs={{0,4},{4,0},{1,5},{5,1},{2,6},{6,2},{3,7},{7,3},{8,12},{12,8},{9,1... | collective-permute-start | bytes 393224 | tf_op jit(solution)/shard_map/ppermute | solution.py:21
  19.2 2.9 %copy-start.22 = (bf16[128,2,256]{2,0,1:T(8,128)(2,1)}, bf16[128,2,256]{2,0,1:T(8,128)(2,1)S(1)}, u32[]{:S(2)}) copy-start(bf16[128,2,256]{2,0,1:T(8,128)(2,1)S(1)} %collective-permute-done.3) | copy-start | bytes 393220
  19.4 8.0 %collective-permute-start.4 = (bf16[128,2,256]{2,0,1:T(8,128)(2,1)S(1)}, bf16[128,2,256]{2,0,1:T(8,128)(2,1)S(1)}, u32[]{:S(2)}, u32[]{:S(2)}) collective-permute-start(bf16[128,2,256]{2,0,1:T(8,128)(2,1)S(1)} %fusion.18), channel_id=1, source_target_pairs={{0,8},{8,0},{1,9},{9,1},{2,10},{10,2},{3,11},{11,3},{4,12},{12,4},... | collective-permute-start | bytes 393224 | tf_op jit(solution)/shard_map/ppermute | solution.py:21
  27.4 3.0 %copy-start.20 = (bf16[128,2,256]{2,0,1:T(8,128)(2,1)}, bf16[128,2,256]{2,0,1:T(8,128)(2,1)S(1)}, u32[]{:S(2)}) copy-start(bf16[128,2,256]{2,0,1:T(8,128)(2,1)S(1)} %collective-permute-done.4) | copy-start | bytes 393220
  27.6 5.0 %collective-permute-start.5 = (bf16[128,512]{1,0:T(8,128)(2,1)S(1)}, bf16[128,512]{1,0:T(8,128)(2,1)S(1)}, u32[]{:S(2)}, u32[]{:S(2)}) collective-permute-start(bf16[128,512]{1,0:T(8,128)(2,1)S(1)} %bitcast.247), channel_id=1, source_target_pairs={{0,16},{16,0},{1,17},{17,1},{2,18},{18,2},{3,19},{19,3},{4,20},{20... | collective-permute-start | bytes 393224 | tf_op jit(solution)/shard_map/ppermute | solution.py:21
  32.7 156.7 %slice-start = ((s8[7340032]{0:T(1024)(128)(4,1)}), s8[4194304]{0:T(1024)(128)(4,1)S(1)}, s32[]{:S(2)}) async-start(s8[7340032]{0:T(1024)(128)(4,1)} %bitcast.201), calls=%async_computation | async-start | bytes 8388608
  33.4 156.0 %slice-start.1 = ((s8[7340032]{0:T(1024)(128)(4,1)}), s8[3145728]{0:T(1024)(128)(4,1)S(1)}, s32[]{:S(2)}) async-start(s8[7340032]{0:T(1024)(128)(4,1)} %bitcast.201), calls=%async_computation.1 | async-start | bytes 6291456
  189.4 2.1 copy-start.27
  191.5 5.9 %copy-start.19 = (bf16[128,2,256]{0,2,1:T(8,128)(2,1)S(1)}, bf16[128,2,256]{0,2,1:T(8,128)(2,1)}, u32[]{:S(2)}) copy-start(bf16[128,2,256]{0,2,1:T(8,128)(2,1)} %copy.37) | copy-start | bytes 393220
  191.5 6.7 %copy-start.23 = (bf16[128,2,256]{2,0,1:T(8,128)(2,1)S(1)}, bf16[128,2,256]{2,0,1:T(8,128)(2,1)}, u32[]{:S(2)}) copy-start(bf16[128,2,256]{2,0,1:T(8,128)(2,1)} %copy-done.22) | copy-start | bytes 393220
  191.6 11.3 %copy-start.5 = (bf16[1,512,256]{2,1,0:T(8,128)(2,1)S(1)}, bf16[1,512,256]{2,1,0:T(8,128)(2,1)}, u32[]{:S(2)}) copy-start(bf16[1,512,256]{2,1,0:T(8,128)(2,1)} %copy-done.4) | copy-start | bytes 786436
  196.8 9.0 %copy-start.21 = (bf16[128,2,256]{2,0,1:T(8,128)(2,1)S(1)}, bf16[128,2,256]{2,0,1:T(8,128)(2,1)}, u32[]{:S(2)}) copy-start(bf16[128,2,256]{2,0,1:T(8,128)(2,1)} %copy-done.20) | copy-start | bytes 393220
  196.8 15.1 %copy-start.13 = (bf16[1,512,256]{2,1,0:T(8,128)(2,1)S(1)}, bf16[1,512,256]{2,1,0:T(8,128)(2,1)}, u32[]{:S(2)}) copy-start(bf16[1,512,256]{2,1,0:T(8,128)(2,1)} %copy-done.12) | copy-start | bytes 786436
  196.8 15.3 %copy-start.3 = (bf16[1,512,256]{2,1,0:T(8,128)(2,1)S(1)}, bf16[1,512,256]{2,1,0:T(8,128)(2,1)}, u32[]{:S(2)}) copy-start(bf16[1,512,256]{2,1,0:T(8,128)(2,1)} %copy-done.2) | copy-start | bytes 786436
  196.9 5.9 %collective-permute-start.7 = (bf16[128,512]{1,0:T(8,128)(2,1)S(1)}, bf16[128,512]{1,0:T(8,128)(2,1)S(1)}, u32[]{:S(2)}, u32[]{:S(2)}) collective-permute-start(bf16[128,512]{1,0:T(8,128)(2,1)S(1)} %slice.145), channel_id=1, source_target_pairs={{0,16},{16,0},{1,17},{17,1},{2,18},{18,2},{3,19},{19,3},{4,20},{20... | collective-permute-start | bytes 393224 | tf_op jit(solution)/shard_map/ppermute | solution.py:21
  203.0 8.8 %collective-permute-start.8 = (bf16[128,2,256]{2,0,1:T(8,128)(2,1)S(1)}, bf16[128,2,256]{2,0,1:T(8,128)(2,1)S(1)}, u32[]{:S(2)}, u32[]{:S(2)}) collective-permute-start(bf16[128,2,256]{2,0,1:T(8,128)(2,1)S(1)} %fusion.13), channel_id=1, source_target_pairs={{0,8},{8,0},{1,9},{9,1},{2,10},{10,2},{3,11},{11,3},{4,12},{12,4},... | collective-permute-start | bytes 393224 | tf_op jit(solution)/shard_map/ppermute | solution.py:21
  206.6 38.8 %collective-permute-start.12 = (bf16[128,4608]{0,1:T(8,128)(2,1)}, bf16[128,4608]{0,1:T(8,128)(2,1)}, u32[]{:S(2)}, u32[]{:S(2)}) collective-permute-start(bf16[128,4608]{0,1:T(8,128)(2,1)} %constant_dynamic-update-slice_fusion), channel_id=1, source_target_pairs={{0,16},{16,0},{1,17},{17,1},{2,18},{18,2},{3,19},{19,3},{4,20},{20... | collective-permute-start | bytes 3538952 | tf_op jit(solution)/shard_map/ppermute | solution.py:21
  212.4 8.7 %collective-permute-start.9 = (bf16[128,2,256]{2,0,1:T(8,128)(2,1)S(1)}, bf16[128,2,256]{2,0,1:T(8,128)(2,1)S(1)}, u32[]{:S(2)}, u32[]{:S(2)}) collective-permute-start(bf16[128,2,256]{2,0,1:T(8,128)(2,1)S(1)} %fusion.14), channel_id=1, source_target_pairs={{0,4},{4,0},{1,5},{5,1},{2,6},{6,2},{3,7},{7,3},{8,12},{12,8},{9,1... | collective-permute-start | bytes 393224 | tf_op jit(solution)/shard_map/ppermute | solution.py:21
  212.5 8.5 %copy-start.11 = (bf16[1,512,256]{2,1,0:T(8,128)(2,1)S(1)}, bf16[1,512,256]{2,1,0:T(8,128)(2,1)}, u32[]{:S(2)}) copy-start(bf16[1,512,256]{2,1,0:T(8,128)(2,1)} %copy-done.10) | copy-start | bytes 786436
  212.5 26.4 %copy-start.9 = (bf16[1,512,256]{2,1,0:T(8,128)(2,1)S(1)}, bf16[1,512,256]{2,1,0:T(8,128)(2,1)}, u32[]{:S(2)}) copy-start(bf16[1,512,256]{2,1,0:T(8,128)(2,1)} %copy-done.8) | copy-start | bytes 786436
  218.8 20.4 %copy-start.1 = (bf16[1,512,256]{2,1,0:T(8,128)(2,1)S(1)}, bf16[1,512,256]{2,1,0:T(8,128)(2,1)}, u32[]{:S(2)}) copy-start(bf16[1,512,256]{2,1,0:T(8,128)(2,1)} %copy-done) | copy-start | bytes 786436
  218.9 23.4 %copy-start.7 = (bf16[1,512,256]{2,1,0:T(8,128)(2,1)S(1)}, bf16[1,512,256]{2,1,0:T(8,128)(2,1)}, u32[]{:S(2)}) copy-start(bf16[1,512,256]{2,1,0:T(8,128)(2,1)} %copy-done.6) | copy-start | bytes 786436
  218.9 19.4 %collective-permute-start.6 = (bf16[128,512]{1,0:T(8,128)(2,1)S(1)}, bf16[128,512]{1,0:T(8,128)(2,1)S(1)}, u32[]{:S(2)}, u32[]{:S(2)}) collective-permute-start(bf16[128,512]{1,0:T(8,128)(2,1)S(1)} %slice.146), channel_id=1, source_target_pairs={{0,16},{16,0},{1,17},{17,1},{2,18},{18,2},{3,19},{19,3},{4,20},{20... | collective-permute-start | bytes 393224 | tf_op jit(solution)/shard_map/ppermute | solution.py:21
  219.5 20.6 %collective-permute-start.17 = (bf16[128,2,256]{2,0,1:T(8,128)(2,1)S(1)}, bf16[128,2,256]{2,0,1:T(8,128)(2,1)S(1)}, u32[]{:S(2)}, u32[]{:S(2)}) collective-permute-start(bf16[128,2,256]{2,0,1:T(8,128)(2,1)S(1)} %bitcast.250), channel_id=1, source_target_pairs={{0,16},{16,0},{1,17},{17,1},{2,18},{18,2},{3,19},{19,3},{4,20},{20... | collective-permute-start | bytes 393224 | tf_op jit(solution)/shard_map/ppermute | solution.py:21
  221.5 17.4 %collective-permute-start.10 = (bf16[128,2,256]{2,0,1:T(8,128)(2,1)S(1)}, bf16[128,2,256]{2,0,1:T(8,128)(2,1)S(1)}, u32[]{:S(2)}, u32[]{:S(2)}) collective-permute-start(bf16[128,2,256]{2,0,1:T(8,128)(2,1)S(1)} %fusion.15), channel_id=1, source_target_pairs={{0,2},{2,0},{1,3},{3,1},{4,6},{6,4},{5,7},{7,5},{8,10},{10,8},{9,1... | collective-permute-start | bytes 393224 | tf_op jit(solution)/shard_map/ppermute | solution.py:21
  239.4 2.8 %collective-permute-start.11 = (bf16[128,2,256]{2,0,1:T(8,128)(2,1)S(1)}, bf16[128,2,256]{2,0,1:T(8,128)(2,1)S(1)}, u32[]{:S(2)}, u32[]{:S(2)}) collective-permute-start(bf16[128,2,256]{2,0,1:T(8,128)(2,1)S(1)} %fusion.16), channel_id=1, source_target_pairs={{0,1},{1,0},{2,3},{3,2},{4,5},{5,4},{6,7},{7,6},{8,9},{9,8},{10,11... | collective-permute-start | bytes 393224 | tf_op jit(solution)/shard_map/ppermute | solution.py:21
  239.5 19.3 %collective-permute-start.16 = (bf16[128,2,256]{2,0,1:T(8,128)(2,1)S(1)}, bf16[128,2,256]{2,0,1:T(8,128)(2,1)S(1)}, u32[]{:S(2)}, u32[]{:S(2)}) collective-permute-start(bf16[128,2,256]{2,0,1:T(8,128)(2,1)S(1)} %add_convert_fusion), channel_id=1, source_target_pairs={{0,16},{16,0},{1,17},{17,1},{2,18},{18,2},{3,19},{19,3},{4,20},{20... | collective-permute-start | bytes 393224 | tf_op jit(solution)/shard_map/ppermute | solution.py:21
  240.1 5.3 %copy-start.14 = (bf16[256,2,256]{2,0,1:T(8,128)(2,1)}, bf16[256,2,256]{2,0,1:T(8,128)(2,1)S(1)}, u32[]{:S(2)}) copy-start(bf16[256,2,256]{2,0,1:T(8,128)(2,1)S(1)} %constant_dynamic-update-slice_fusion.9) | copy-start | bytes 786436
  240.1 17.4 %collective-permute-start.15 = (bf16[128,2,256]{2,0,1:T(8,128)(2,1)S(1)}, bf16[128,2,256]{2,0,1:T(8,128)(2,1)}, u32[]{:S(2)}, u32[]{:S(2)}) collective-permute-start(bf16[128,2,256]{2,0,1:T(8,128)(2,1)S(1)} %fusion.9), channel_id=1, source_target_pairs={{0,16},{16,0},{1,17},{17,1},{2,18},{18,2},{3,19},{19,3},{4,20},{20... | collective-permute-start | bytes 393224 | tf_op jit(solution)/shard_map/ppermute | solution.py:21
  241.7 14.6 %collective-permute-start.14 = (bf16[128,2,256]{2,0,1:T(8,128)(2,1)S(1)}, bf16[128,2,256]{2,0,1:T(8,128)(2,1)}, u32[]{:S(2)}, u32[]{:S(2)}) collective-permute-start(bf16[128,2,256]{2,0,1:T(8,128)(2,1)S(1)} %fusion.10), channel_id=1, source_target_pairs={{0,16},{16,0},{1,17},{17,1},{2,18},{18,2},{3,19},{19,3},{4,20},{20... | collective-permute-start | bytes 393224 | tf_op jit(solution)/shard_map/ppermute | solution.py:21
  242.5 11.6 %collective-permute-start.13 = (bf16[128,2,256]{2,0,1:T(8,128)(2,1)S(1)}, bf16[128,2,256]{2,0,1:T(8,128)(2,1)}, u32[]{:S(2)}, u32[]{:S(2)}) collective-permute-start(bf16[128,2,256]{2,0,1:T(8,128)(2,1)S(1)} %fusion.11), channel_id=1, source_target_pairs={{0,16},{16,0},{1,17},{17,1},{2,18},{18,2},{3,19},{19,3},{4,20},{20... | collective-permute-start | bytes 393224 | tf_op jit(solution)/shard_map/ppermute | solution.py:21
  245.4 2.7 %copy-start.15 = (bf16[256,2,256]{2,0,1:T(8,128)(2,1)S(1)}, bf16[256,2,256]{2,0,1:T(8,128)(2,1)}, u32[]{:S(2)}) copy-start(bf16[256,2,256]{2,0,1:T(8,128)(2,1)} %copy-done.14) | copy-start | bytes 786436
  248.1 7.0 %copy-start.18 = (bf16[256,1,2,256]{0,3,2,1:T(8,128)(2,1)S(1)}, bf16[256,1,2,256]{0,3,2,1:T(8,128)(2,1)}, u32[]{:S(2)}) copy-start(bf16[256,1,2,256]{0,3,2,1:T(8,128)(2,1)} %reverse.4) | copy-start | bytes 786436
  261.8 1.5 copy-start.25
  261.8 2.3 copy-start.26
